TPU v7x, 128 devices: a whole 4x4x4 slice. The times are simulated.
128 devices in a mesh: lat: 8 (over z_lo, y), lon: 16 (over x, z_hi, core).
Axes of the slice: x: 4, y: 4, z: 4 (z_hi: 2, z_lo: 2; z = z_hi * 2 + z_lo), core: 2. Of those that a mesh axis runs over, the one named last changes fastest.
Arguments:
- warmth_offset: float32 [8, 512, 2048], P(None, 'lat', 'lon'), may hold values from -8 to 8
- saltiness_offset: float32 [8, 512, 2048], P(None, 'lat', 'lon'), may hold values from -2.5 to 2.5
- easterly_speed_field: float32 [8, 512, 2048], P(None, 'lat', 'lon'), may hold values from -2.5 to 2.5
- northerly_speed_field: float32 [8, 512, 2048], P(None, 'lat', 'lon'), may hold values from -2.5 to 2.5
- east_west_spacing: float32 [512, 2048], P('lat', 'lon'), may hold values from 0.7 to 1.4
- north_south_spacing: float32 [512, 2048], P('lat', 'lon'), may hold values from 0.7 to 1.4
- layer_depth_span: float32 [8, 512, 2048], P(None, 'lat', 'lon'), may hold values from 0.7 to 1.4
- water_indicator: int32 [8, 512, 2048], P(None, 'lat', 'lon'), may hold values 0 or 1
- hinge_category: int32 [1], replicated, may hold values from 0 to 1
Outputs:
- temperature_next: float32 [8, 512, 2048], P(None, 'lat', 'lon')
- salinity_next: float32 [8, 512, 2048], P(None, 'lat', 'lon')
- zonal_next: float32 [8, 512, 2048], P(None, 'lat', 'lon')
- north_next: float32 [8, 512, 2048], P(None, 'lat', 'lon')
- density: float32 [8, 512, 2048], P(None, 'lat', 'lon')
Inputs may be any that keep to these rules, and one draw needn't show every extreme that they name: `water_indicator`: 1 marks sea, 0 land. `hinge_category`: 0: the row beyond the north edge mirrors the top row; 1: it mirrors the row below the top row.
All inputs are finite; a program needn't handle non-finite values. No bound on the sum of `water_indicator` on one device may be relied on, other than what follows from the above.
Results may differ from a plain program's by a relative error of at most 0.0003.
Values sent between devices are 32-bit elements; how exact they have to be, the bound alone decides.
No kernel may reach another device: no remote copies, remote signals or barrier semaphores. Data moves between devices by JAX's collectives and lax.ppermute only.
A program may use at most 64 MiB of HBM per device.

v0:
```python
import jax
import jax.numpy as jnp
from jax import lax
from jax.experimental import pallas as pl
from jax.experimental.pallas import tpu as pltpu
from jax.sharding import PartitionSpec as P

F32 = jnp.float32
NSTEP = 4
LEVELS = 8
ROWS = 64
LANES = 128
HALO = 4
BLOCK = 9
GROUP = 16

time_step = 0.2
diffusivity = 0.4
eos_alpha = 0.1655
eos_beta = 0.76554
eos_lambda_one = 0.05952
eos_lambda_two = 0.00054914
eos_mu_one = 0.0001497
eos_mu_two = 1.109e-05
eos_cross = 0.0024341

SIGNS = (1.0, 1.0, -1.0, -1.0)
VMEM_LIMIT = 40 * 1024 * 1024


def roll(x, shift):
    shift = shift % LANES
    return pltpu.roll(x, shift, 1) if shift else x


def lanes():
    return lax.broadcasted_iota(jnp.int32, (LEVELS, LANES), 1)


def levels():
    return lax.broadcasted_iota(jnp.int32, (LEVELS, LANES), 0)


def mirrored(x, width):
    lane = lanes()
    bit = 1
    while bit < width:
        x = jnp.where((lane & bit) != 0, roll(x, bit), roll(x, -bit))
        bit *= 2
    return x


def eos_terms():
    depth = 100.0 * (levels().astype(F32) + 0.5)
    return -eos_alpha * (1.0 + eos_mu_one * depth), eos_beta * (1.0 - eos_mu_two * depth)


def density_of(heat, salt, terms):
    heat_term, salt_term = terms
    return heat * (heat_term - (0.5 * eos_alpha * eos_lambda_one) * heat - eos_cross * salt) + salt * (
        salt_term - (0.5 * eos_beta * eos_lambda_two) * salt
    )


def pressure_of(heat, salt, half_depth, terms):
    half = density_of(heat, salt, terms) * half_depth
    level = levels()
    total = half
    for shift in (1, 2, 4):
        total = total + jnp.where(level >= shift, pltpu.roll(total, shift, 0), 0.0)
    return total + total - half


def geometry_row(geo, row, east0, north0, east1, north1):
    half0 = geo["half"][row]
    half1 = geo["half"][row + 1]
    half_e = roll(half0, -1)
    span = 2.0 / (east0 + roll(east0, -1))
    side = 0.5 * (north0 + roll(north0, -1))
    open_e = jnp.minimum(half0, half_e) > 0.0
    area = jnp.where(open_e, side * (half0 + half_e), 0.0)
    geo["area_e"][row] = area
    geo["cond_e"][row] = diffusivity * area * span
    geo["open_e"][row] = jnp.where(open_e, 1.0, 0.0)
    geo["push_e"][row] = time_step * span
    span = 2.0 / (north0 + north1)
    side = 0.5 * (east0 + east1)
    open_n = jnp.minimum(half0, half1) > 0.0
    area = jnp.where(open_n, side * (half0 + half1), 0.0)
    geo["area_n"][row] = area
    geo["cond_n"][row] = diffusivity * area * span
    geo["open_n"][row] = jnp.where(open_n, 1.0, 0.0)
    geo["push_n"][row] = time_step * span
    geo["inv"][row] = (0.5 * time_step) / (east0 * north0 * jnp.where(half0 > 0.0, half0, 1.0))


def march(state, geo, bases, low, blocks, unroll):
    terms = eos_terms()

    def north_face(row, speed):
        flow = geo["area_n"][row] * speed
        ahead = jnp.maximum(flow, 0.0) + geo["cond_n"][row]
        return ahead, flow - ahead

    def first(base):
        row = base + low
        before = tuple(ref[row - 1] for ref in state)
        here = tuple(ref[row] for ref in state)
        return before + here + north_face(row - 1, before[3]) + (pressure_of(here[0], here[1], geo["half"][row], terms),)

    def block(index, carries):
        start = low + index * unroll
        nexts = [[tuple(ref[base + start + u + 1] for ref in state) for u in range(unroll)] for base in bases]
        after = []
        stores = []
        for base, ahead_rows, carry in zip(bases, nexts, carries):
            before, here = carry[0:4], carry[4:8]
            south_p, south_m, press = carry[8:]
            for u in range(unroll):
                row = base + start + u
                north = ahead_rows[u]
                press_n = pressure_of(north[0], north[1], geo["half"][row + 1], terms)
                north_p, north_m = north_face(row, here[3])
                flow = geo["area_e"][row] * here[2]
                east_p = jnp.maximum(flow, 0.0) + geo["cond_e"][row]
                east_m = flow - east_p
                west_p, west_m = roll(east_p, 1), roll(east_m, 1)
                inv = geo["inv"][row]
                keep = 1.0 - inv * ((east_p - west_m) + (north_p - south_m))
                c_e, c_w, c_n, c_s = inv * east_m, inv * west_p, inv * north_m, inv * south_p
                new = [
                    keep * c + (c_w * roll(c, 1) + c_s * s) - (c_e * roll(c, -1) + c_n * n)
                    for c, s, n in zip(here, before, north)
                ]
                new[2] = (new[2] + (press - roll(press, -1)) * geo["push_e"][row]) * geo["open_e"][row]
                new[3] = (new[3] + (press - press_n) * geo["push_n"][row]) * geo["open_n"][row]
                stores.append((row, new))
                before, here = here, north
                south_p, south_m, press = north_p, north_m, press_n
            after.append(before + here + (south_p, south_m, press))
        for row, new in stores:
            for ref, value in zip(state, new):
                ref[row] = value
        return tuple(after)

    lax.fori_loop(0, blocks, block, tuple(first(base) for base in bases))


GEO = ("half", "area_e", "cond_e", "open_e", "push_e", "area_n", "cond_n", "open_n", "push_n", "inv")


def geo_scratch(rows):
    return [pltpu.VMEM((rows, LEVELS, LANES), F32) for _ in GEO]


def column_of(ref, row):
    return ref[pl.ds(row, LEVELS, stride=ROWS), :]


def wide(ref, row):
    return jnp.broadcast_to(ref[pl.ds(row, 1), :], (LEVELS, LANES))


def own_row(refs, row):
    heat, salt, east, north, thick, water = [column_of(ref, row) for ref in refs[:6]]
    wet = water.astype(F32)
    return heat * wet, salt * wet, east, north, 0.5 * (thick * wet)


def rows_kernel(*refs):
    ins, (out_a, out_b) = refs[:8], refs[8:]
    even = lax.rem(lax.axis_index("lat"), 2) == 0
    start_a = jnp.where(even, ROWS - HALO, 0)
    start_b = jnp.where(even, 0, ROWS - HALO - 1)
    out_b[25] = jnp.ones((LEVELS, LANES), F32)
    out_b[26] = jnp.ones((LEVELS, LANES), F32)
    for i in range(HALO):
        for f, value in enumerate(own_row(ins, start_a + i)):
            out_a[5 * i + f] = value
        out_a[20, pl.ds(i, 1), :] = ins[6][pl.ds(start_a + i, 1), :]
        out_a[20, pl.ds(HALO + i, 1), :] = ins[7][pl.ds(start_a + i, 1), :]
    for i in range(HALO + 1):
        for f, value in enumerate(own_row(ins, start_b + i)):
            out_b[5 * i + f] = value
        out_b[25, pl.ds(i, 1), :] = ins[6][pl.ds(start_b + i, 1), :]
        out_b[26, pl.ds(i, 1), :] = ins[7][pl.ds(start_b + i, 1), :]


def halo_rows(got_a, got_b):
    even = lax.rem(lax.axis_index("lat"), 2) == 0

    def spread(row):
        return jnp.broadcast_to(row, (LEVELS, LANES))

    def read_a(i, f):
        if f < 5:
            return got_a[5 * i + f]
        return spread(got_a[20, pl.ds(HALO * (f - 5) + i, 1), :])

    def read_b(i, f):
        if f < 5:
            return got_b[5 * i + f]
        return spread(got_b[20 + f, pl.ds(i, 1), :])

    def sane(value, f):
        return value if f < 5 else jnp.where(value > 0.0, value, 1.0)

    def south(i, f):
        return sane(jnp.where(even, read_b(i + 1, f), read_a(i, f)), f)

    def north(i, f):
        return sane(jnp.where(even, read_a(i, f), read_b(i, f)), f)

    def fold(i, f):
        return sane(read_b(i, f), f)

    return south, north, fold


def interior_kernel(*refs):
    ins = refs[:8]
    state_out, own, msgs = refs[8:11]
    state = [state_out.at[f] for f in range(4)]
    geo = dict(zip(GEO, refs[11:]))

    def take(row, carry):
        values = own_row(ins, row)
        for ref, value in zip(state, values):
            ref[row] = value
        geo["half"][row] = values[4]
        return carry

    lax.fori_loop(0, ROWS, take, 0)

    lane = lanes()
    part = (lane // HALO) % (GROUP // HALO)

    def pack(g, carry):
        packs = []
        for f in range(7):
            west = east = jnp.zeros((LEVELS, LANES), F32)
            for q in range(8):
                row = jnp.clip(BLOCK * q + g - HALO, 0, ROWS - 1)
                if f < 4:
                    value = state[f][row]
                elif f == 4:
                    value = geo["half"][row]
                else:
                    value = wide(ins[f + 1], row)
                here = (lane // GROUP) == q
                west = jnp.where(here, roll(value, GROUP * q + HALO), west)
                east = jnp.where(here, roll(value, GROUP * q + 12), east)
            own[0, f, g] = west
            own[1, f, g] = east
            packs.append((west, east))
        for side in range(2):
            for half, first in ((0, 0), (1, 4)):
                message = jnp.zeros((LEVELS, LANES), F32)
                for f in range(4 if half == 0 else 3):
                    value = packs[first + f][side]
                    shift = HALO * f - (HALO if side == 0 else 2 * HALO)
                    message = jnp.where(part == f, roll(value, shift), message)
                msgs[side, BLOCK * half + g] = message
        return carry

    lax.fori_loop(0, BLOCK, pack, 0)

    def shape(row, carry):
        geometry_row(geo, row, wide(ins[6], row), wide(ins[7], row), wide(ins[6], row + 1), wide(ins[7], row + 1))
        return carry

    lax.fori_loop(0, ROWS - 1, shape, 0)

    def step(s, carry):
        march(state, geo, (0,), s, 32 - s, 2)
        return carry

    lax.fori_loop(1, NSTEP + 1, step, 0)


def columns_kernel(msgs, got_a, got_b, out_a, out_b):
    even = lax.rem(lax.axis_index("lon"), 2) == 0
    top = lax.axis_index("lat") == lax.axis_size("lat") - 1
    south, north, fold = halo_rows(got_a, got_b)
    lane = lanes()
    part = (lane // HALO) % (GROUP // HALO)
    for half, first in ((0, 0), (1, 4)):
        for g in range(BLOCK):
            slot = BLOCK * half + g
            west, east = msgs[0, slot], msgs[1, slot]
            if g != HALO:
                add_w = add_e = jnp.zeros((LEVELS, LANES), F32)
                base = 0 if g < HALO else 7 * GROUP
                for f in range(4 if half == 0 else 3):
                    if g < HALO:
                        value = south(g, first + f)
                    else:
                        value = jnp.where(top, fold(g - 4, first + f), north(g - 5, first + f))
                    add_w = jnp.where(part == f, roll(value, base + HALO * f), add_w)
                    add_e = jnp.where(part == f, roll(value, base + HALO * f + HALO), add_e)
                if g < HALO:
                    here = lane < GROUP
                else:
                    here = lane >= 7 * GROUP
                    add_w, add_e = jnp.where(top, add_e, add_w), jnp.where(top, add_w, add_e)
                west = jnp.where(here, add_w, west)
                east = jnp.where(here, add_e, east)
            out_a[slot] = jnp.where(even, east, west)
            out_b[slot] = jnp.where(even, west, east)


SOUTH, NORTH, FOLD, NS_ROWS = 0, 12, 24, 30


def rows_strip_kernel(*refs):
    ins = refs[:8]
    got_a, got_b, hinge, out = refs[8:12]
    state = refs[12:16]
    east_w, north_w = refs[16:18]
    geo = dict(zip(GEO, refs[18:]))
    top = lax.axis_index("lat") == lax.axis_size("lat") - 1
    pivot = hinge[0]
    south, north, fold = halo_rows(got_a, got_b)
    fields = list(state) + [geo["half"], east_w, north_w]
    for i in range(HALO):
        for f, ref in enumerate(fields):
            ref[SOUTH + i] = south(i, f)
            ref[NORTH + 8 + i] = north(i, f)
    for i in range(8):
        for base, row in ((SOUTH + HALO, i), (NORTH, ROWS - 8 + i)):
            for ref, value in zip(fields, own_row(ins, row) + (wide(ins[6], row), wide(ins[7], row))):
                ref[base + i] = value

    def refold(ref, sign):
        ghost = sign * mirrored(ref[FOLD + 4 - pivot], LANES)
        ref[FOLD + 5] = sign * mirrored(ref[NORTH + 7 - pivot], LANES)
        ref[NORTH + 8] = ghost

    def shape(row, carry):
        geometry_row(geo, row, east_w[row], north_w[row], east_w[row + 1], north_w[row + 1])
        return carry

    @pl.when(top)
    def _():
        for i in range(HALO + 1):
            for f, ref in enumerate(fields):
                ref[FOLD + i] = fold(i, f)
        for ref in fields[4:]:
            refold(ref, 1.0)
        lax.fori_loop(FOLD, FOLD + 5, shape, 0)

    lax.fori_loop(SOUTH, SOUTH + 11, shape, 0)
    lax.fori_loop(NORTH, NORTH + 11, shape, 0)

    def step(s, carry):
        @pl.when(top)
        def _():
            for ref, sign in zip(state, SIGNS):
                refold(ref, sign)
            march(state, geo, (FOLD,), s, 5 - s, 1)

        march(state, geo, (SOUTH, NORTH), s, 6 - s, 2)
        return carry

    lax.fori_loop(1, NSTEP + 1, step, 0)
    for f, ref in enumerate(state):
        for i in range(HALO):
            out[f, i] = ref[SOUTH + HALO + i]
            out[f, HALO + i] = ref[NORTH + HALO + i]


WEST, EAST, FOLDS, WE_ROWS = 0, 11, 22, 28


def columns_strip_kernel(*refs):
    own, lon_a, lon_b, got_a, got_b, inner, strips, hinge = refs[:8]
    outs = refs[8:13]
    state = refs[13:17]
    east_w, north_w = refs[17:19]
    geo = dict(zip(GEO, refs[19:]))
    even = lax.rem(lax.axis_index("lon"), 2) == 0
    top = lax.axis_index("lat") == lax.axis_size("lat") - 1
    pivot = hinge[0]
    south, north, fold = halo_rows(got_a, got_b)
    fields = list(state) + [geo["half"], east_w, north_w]
    lane = lanes()
    inside = lane % GROUP

    def message(side, f, g):
        slot = g if f < 4 else BLOCK + g
        a, b = lon_a[slot], lon_b[slot]
        return jnp.where(even, b, a) if side == 0 else jnp.where(even, a, b)

    for g in range(BLOCK):
        for f, ref in enumerate(fields):
            west, east = own[0, f, g], own[1, f, g]
            if g < HALO:
                value = south(g, f)
                west = jnp.where(lane < GROUP, roll(value, HALO), west)
                east = jnp.where(lane < GROUP, roll(value, 12), east)
            elif g > HALO:
                value = north(g - 5, f)
                west = jnp.where(lane >= 7 * GROUP, roll(value, 7 * GROUP + HALO), west)
                east = jnp.where(lane >= 7 * GROUP, roll(value, 7 * GROUP + 12), east)
            shift = -HALO * (f % 4)
            west = jnp.where(inside < HALO, roll(message(0, f, g), shift), west)
            east = jnp.where(inside >= 12, roll(message(1, f, g), shift + 12), east)
            if f > 4:
                west = jnp.where(west > 0.0, west, 1.0)
                east = jnp.where(east > 0.0, east, 1.0)
            ref[WEST + 1 + g] = west
            ref[EAST + 1 + g] = east

    def rewrap(ref):
        for base in (WEST, EAST):
            ref[base] = roll(ref[base + 9], GROUP)
            ref[base + 10] = roll(ref[base + 1], -GROUP)

    def refold(ref, sign):
        ghost = sign * mirrored(ref[FOLDS + 4 - pivot], GROUP)
        from_e, from_w = ref[EAST + 5 - pivot], ref[WEST + 5 - pivot]
        back = jnp.where(lane < GROUP, roll(from_e, GROUP), roll(from_w, 2 * GROUP))
        ref[FOLDS + 5] = sign * mirrored(back, GROUP)
        here = lane >= 7 * GROUP
        ref[WEST + 6] = jnp.where(here, roll(ghost, 6 * GROUP), ref[WEST + 6])
        ref[EAST + 6] = jnp.where(here, roll(ghost, 7 * GROUP), ref[EAST + 6])

    def shape(row, carry):
        geometry_row(geo, row, east_w[row], north_w[row], east_w[row + 1], north_w[row + 1])
        return carry

    @pl.when(top)
    def _():
        for i in range(HALO + 1):
            for f, ref in enumerate(fields):
                value = fold(i, f)
                value = jnp.where(lane < GROUP, roll(value, HALO), roll(value, 28))
                if i > 0:
                    slot = HALO + i
                    corner = 7 * GROUP + HALO * (f % 4)
                    value = jnp.where(lane < HALO, roll(message(1, f, slot), -corner), value)
                    other = roll(message(0, f, slot), 28 - corner)
                    value = jnp.where((lane >= 28) & (lane < 32), other, value)
                if f > 4:
                    value = jnp.where(value > 0.0, value, 1.0)
                ref[FOLDS + i] = value
        for ref in fields[4:]:
            refold(ref, 1.0)

    for ref in fields[4:]:
        rewrap(ref)

    lax.fori_loop(WEST, WEST + 10, shape, 0)
    lax.fori_loop(EAST, EAST + 10, shape, 0)

    @pl.when(top)
    def _():
        lax.fori_loop(FOLDS, FOLDS + 5, shape, 0)

    def step(s, carry):
        @pl.when(top)
        def _():
            for ref, sign in zip(state, SIGNS):
                refold(ref, sign)
            march(state, geo, (FOLDS,), s, 5 - s, 1)

        for ref in state:
            rewrap(ref)
        march(state, geo, (WEST, EAST), 1, 3, 3)
        return carry

    lax.fori_loop(1, NSTEP + 1, step, 0)

    for ref in state:
        for g in range(BLOCK):
            ref[WEST + 1 + g] = jnp.where(inside < HALO, roll(ref[EAST + 1 + g], -8), ref[WEST + 1 + g])
    rim = (lane < HALO) | (lane >= LANES - HALO)
    terms = eos_terms()

    def emit(row, bases, q, g):
        new = [
            jnp.where(rim, roll(ref[WEST + 1 + g], -(GROUP * q + HALO)), base) for ref, base in zip(state, bases)
        ]
        new.append(density_of(new[0], new[1], terms))
        for ref, value in zip(outs, new):
            ref[pl.ds(row, LEVELS, stride=ROWS), :] = value

    for i in range(HALO):
        emit(i, [strips[f, i] for f in range(4)], 0, HALO + i)
        emit(ROWS - HALO + i, [strips[f, HALO + i] for f in range(4)], 7, 1 + i)
    emit(HALO, [inner[f, HALO] for f in range(4)], 0, 8)
    emit(ROWS - HALO - 1, [inner[f, ROWS - HALO - 1] for f in range(4)], 7, 0)

    def merge(g, carry):
        for q in range(1, 7):
            row = BLOCK * q + g - HALO
            emit(row, [inner[f, row] for f in range(4)], q, g)
        return carry

    lax.fori_loop(0, BLOCK, merge, 0)


def call(kernel, ins, outs, scratch=(), smem_last=False, flops=0):
    specs = [pl.BlockSpec(memory_space=pltpu.VMEM) for _ in ins]
    if smem_last:
        specs[-1] = pl.BlockSpec(memory_space=pltpu.SMEM)
    return pl.pallas_call(
        kernel,
        out_shape=[jax.ShapeDtypeStruct(shape, F32) for shape in outs],
        in_specs=specs,
        out_specs=[pl.BlockSpec(memory_space=pltpu.VMEM) for _ in outs],
        scratch_shapes=list(scratch),
        compiler_params=pltpu.CompilerParams(vmem_limit_bytes=VMEM_LIMIT),
        cost_estimate=pl.CostEstimate(flops=flops, bytes_accessed=2_000_000, transcendentals=0),
    )(*ins)


def lat_pairs(lat, lon):
    first = [(a * lon + o, (a ^ 1) * lon + o) for a in range(lat) for o in range(lon)]
    second = [
        (a * lon + o, (a + 1 if a % 2 else a - 1) * lon + o) for a in range(1, lat - 1) for o in range(lon)
    ]
    second += [((lat - 1) * lon + o, (lat - 1) * lon + lon - 1 - o) for o in range(lon)]
    return first, second


def lon_pairs(lat, lon):
    first = [(a * lon + o, a * lon + (o ^ 1)) for a in range(lat) for o in range(lon)]
    second = [
        (a * lon + o, a * lon + ((o + 1) if o % 2 else (o - 1)) % lon) for a in range(lat) for o in range(lon)
    ]
    return first, second


def on_device(*args):
    lat, lon = lax.axis_size("lat"), lax.axis_size("lon")
    axes = ("lat", "lon")
    flat = [x.reshape(LEVELS * ROWS, LANES) for x in (*args[:4], args[6], args[7])]
    ins = flat + [args[4], args[5]]
    hinge = args[8]
    tile = (LEVELS, LANES)
    state_scratch = lambda rows: [pltpu.VMEM((rows,) + tile, F32) for _ in range(6)]

    rows_a, rows_b = call(rows_kernel, ins, [(21,) + tile, (27,) + tile])
    pairs_a, pairs_b = lat_pairs(lat, lon)
    got_b = lax.ppermute(rows_b, axes, pairs_b)
    got_a = lax.ppermute(rows_a, axes, pairs_a)
    inner, own, msgs = call(
        interior_kernel,
        ins,
        [(4, ROWS) + tile, (2, 7, BLOCK) + tile, (2, 2 * BLOCK) + tile],
        geo_scratch(ROWS),
        flops=40_000_000,
    )
    cols_a, cols_b = call(columns_kernel, [msgs, got_a, got_b], [(2 * BLOCK,) + tile] * 2)
    pairs_a, pairs_b = lon_pairs(lat, lon)
    lon_b = lax.ppermute(cols_b, axes, pairs_b)
    lon_a = lax.ppermute(cols_a, axes, pairs_a)
    (strips,) = call(
        rows_strip_kernel,
        ins + [got_a, got_b, hinge],
        [(4, 2 * HALO) + tile],
        state_scratch(NS_ROWS) + geo_scratch(NS_ROWS),
        smem_last=True,
        flops=10_000_000,
    )
    outs = call(
        columns_strip_kernel,
        [own, lon_a, lon_b, got_a, got_b, inner, strips, hinge],
        [(LEVELS * ROWS, LANES)] * 5,
        state_scratch(WE_ROWS) + geo_scratch(WE_ROWS),
        smem_last=True,
        flops=10_000_000,
    )
    return tuple(x.reshape(LEVELS, ROWS, LANES) for x in outs)


def solution(mesh):
    field = P(None, "lat", "lon")
    flat = P("lat", "lon")
    return jax.shard_map(
        on_device,
        mesh=mesh,
        in_specs=(field, field, field, field, flat, flat, field, field, P()),
        out_specs=(field,) * 5,
        check_vma=False,
    )
```

profile of v0, /device:TPU:56, one launch (start us, length us, event | category | flops | bytes accessed | tf_op | source)
XLA Modules:
  0.0 55.1 jit_solution(11810221555365068075)
XLA Ops:
  0.6 0.0 copy-start
  0.6 0.9 %copy-done = f32[8,64,128]{2,1,0:T(8,128)S(1)} copy-done((f32[8,64,128]{2,1,0:T(8,128)S(1)}, f32[8,64,128]{2,1,0:T(8,128)}, u32[]{:S(2)}) %copy-start) | copy-done | bytes 262168
  1.6 0.0 copy-start.2
  1.6 0.9 %copy-done.2 = f32[8,64,128]{2,1,0:T(8,128)S(1)} copy-done((f32[8,64,128]{2,1,0:T(8,128)S(1)}, f32[8,64,128]{2,1,0:T(8,128)}, u32[]{:S(2)}) %copy-start.2) | copy-done | bytes 262168
  2.5 0.0 copy-start.4
  2.5 0.9 %copy-done.4 = f32[8,64,128]{2,1,0:T(8,128)S(1)} copy-done((f32[8,64,128]{2,1,0:T(8,128)S(1)}, f32[8,64,128]{2,1,0:T(8,128)}, u32[]{:S(2)}) %copy-start.4) | copy-done | bytes 262168
  3.5 0.0 copy-start.5
  3.5 0.9 %copy-done.5 = f32[8,64,128]{2,1,0:T(8,128)S(1)} copy-done((f32[8,64,128]{2,1,0:T(8,128)S(1)}, f32[8,64,128]{2,1,0:T(8,128)}, u32[]{:S(2)}) %copy-start.5) | copy-done | bytes 262168
  4.4 0.0 copy-start.6
  4.4 0.9 %copy-done.6 = f32[8,64,128]{2,1,0:T(8,128)S(1)} copy-done((f32[8,64,128]{2,1,0:T(8,128)S(1)}, f32[8,64,128]{2,1,0:T(8,128)}, u32[]{:S(2)}) %copy-start.6) | copy-done | bytes 262168
  5.4 0.0 copy-start.7
  5.4 0.9 %copy-done.7 = s32[8,64,128]{2,1,0:T(8,128)S(1)} copy-done((s32[8,64,128]{2,1,0:T(8,128)S(1)}, s32[8,64,128]{2,1,0:T(8,128)}, u32[]{:S(2)}) %copy-start.7) | copy-done | bytes 262168
  6.3 0.0 copy-start.8
  6.3 0.8 %copy-done.8 = f32[64,128]{1,0:T(8,128)S(1)} copy-done((f32[64,128]{1,0:T(8,128)S(1)}, f32[64,128]{1,0:T(8,128)}, u32[]{:S(2)}) %copy-start.8) | copy-done | bytes 32792
  7.1 0.8 %copy-done.9 = f32[64,128]{1,0:T(8,128)S(1)} copy-done((f32[64,128]{1,0:T(8,128)S(1)}, f32[64,128]{1,0:T(8,128)}, u32[]{:S(2)}) %copy-start.9) | copy-done | bytes 32792
  7.9 0.1 shard_map.129
  8.0 6.5 %collective-permute-start.1 = (f32[27,8,128]{2,1,0:T(8,128)S(1)}, f32[27,8,128]{2,1,0:T(8,128)S(1)}, u32[]{:S(2)}, u32[]{:S(2)}) collective-permute-start(f32[27,8,128]{2,1,0:T(8,128)S(1)} %get-tuple-element.20), channel_id=1, source_target_pairs={{16,32},{17,33},{18,34},{19,35},{20,36},{21,37},{22,38},{23,39},{2... | collective-permute-start | bytes 331784 | tf_op jit(solution)/shard_map/ppermute | solution.py:546
  14.5 0.1 collective-permute-start
  14.6 0.0 copy-start.3
  14.6 20.2 %shard_map.128 = (f32[4,64,8,128]{3,2,1,0:T(8,128)S(1)}, f32[2,7,9,8,128]{4,3,2,1,0:T(8,128)S(1)}, f32[2,18,8,128]{3,2,1,0:T(8,128)S(1)}) custom-call(f32[512,128]{1,0:T(8,128)S(1)} %bitcast.12, f32[512,128]{1,0:T(8,128)S(1)} %bitcast.15, f32[512,128]{1,0:T(8,128)S(1)} %bitcast.18, f32[512,128]{1,0:T(8,128)S(1)} %bitcast.21, f32[512,128]{1,0:T(8,128)S(1)} %bitcast.24, ...), custom_call_target="tpu_custom_call" | custom-call | flops 40000000 | bytes 2000000 | tf_op jit(solution)/shard_map/pallas_call | solution.py:507
  34.8 0.0 copy-start.1
  34.8 0.0 collective-permute-done.got_a.refs_8_.refs_3_
  34.9 0.0 collective-permute-done.1.got_b.refs_9_.refs_4_
  34.9 0.2 shard_map.130
  35.1 0.8 %collective-permute-start.2 = (f32[18,8,128]{2,1,0:T(8,128)S(1)}, f32[18,8,128]{2,1,0:T(8,128)S(1)}, u32[]{:S(2)}, u32[]{:S(2)}) collective-permute-start(f32[18,8,128]{2,1,0:T(8,128)S(1)} %get-tuple-element.21), channel_id=1, source_target_pairs={{0,1},{1,0},{2,3},{3,2},{4,5},{5,4},{6,7},{7,6},{8,9},{9,8},{10,11... | collective-permute-start | bytes 221192 | tf_op jit(solution)/shard_map/ppermute | solution.py:558
  35.8 1.2 %collective-permute-start.3 = (f32[18,8,128]{2,1,0:T(8,128)S(1)}, f32[18,8,128]{2,1,0:T(8,128)S(1)}, u32[]{:S(2)}, u32[]{:S(2)}) collective-permute-start(f32[18,8,128]{2,1,0:T(8,128)S(1)} %get-tuple-element.22), channel_id=1, source_target_pairs={{0,15},{1,2},{2,1},{3,4},{4,3},{5,6},{6,5},{7,8},{8,7},{9,10},{10,... | collective-permute-start | bytes 221192 | tf_op jit(solution)/shard_map/ppermute | solution.py:557
  37.6 0.0 copy-done.3
  37.6 0.0 copy-done.1
  37.6 7.6 %shard_map.131.refs_6_ = f32[4,8,8,128]{3,2,1,0:T(8,128)S(1)} custom-call(f32[512,128]{1,0:T(8,128)S(1)} %bitcast.13, f32[512,128]{1,0:T(8,128)S(1)} %bitcast.16, f32[512,128]{1,0:T(8,128)S(1)} %bitcast.19, f32[512,128]{1,0:T(8,128)S(1)} %bitcast.22, f32[512,128]{1,0:T(8,128)S(1)} %bitcast.25, s32[512,128]{1,0:T(8,128)S(1)} %bitcast.28, ...), custom_call_target="tpu_custom_call" | custom-call | flops 10000000 | bytes 2000000 | tf_op jit(solution)/shard_map/pallas_call | solution.py:507
  45.2 0.0 collective-permute-done.2.refs_1_
  45.2 0.0 collective-permute-done.3.refs_2_
  45.2 9.9 %shard_map.132 = (f32[512,128]{1,0:T(8,128)}, f32[512,128]{1,0:T(8,128)}, f32[512,128]{1,0:T(8,128)}, f32[512,128]{1,0:T(8,128)}, f32[512,128]{1,0:T(8,128)}) custom-call(f32[2,7,9,8,128]{4,3,2,1,0:T(8,128)S(1)} %get-tuple-element.17.refs_0_, f32[18,8,128]{2,1,0:T(8,128)S(1)} %collective-permute-done.2.refs_1_, ...), custom_call_target="tpu_custom_call" | custom-call | flops 10000000 | bytes 2000000 | tf_op jit(solution)/shard_map/pallas_call | solution.py:507
  (1 shorter events, 0.0 us)
Async XLA Ops:
  0.6 1.0 %copy-start = (f32[8,64,128]{2,1,0:T(8,128)S(1)}, f32[8,64,128]{2,1,0:T(8,128)}, u32[]{:S(2)}) copy-start(f32[8,64,128]{2,1,0:T(8,128)} %param.9) | copy-start | bytes 786436
  1.6 0.9 %copy-start.2 = (f32[8,64,128]{2,1,0:T(8,128)S(1)}, f32[8,64,128]{2,1,0:T(8,128)}, u32[]{:S(2)}) copy-start(f32[8,64,128]{2,1,0:T(8,128)} %param.10) | copy-start | bytes 786436
  2.5 0.9 %copy-start.4 = (f32[8,64,128]{2,1,0:T(8,128)S(1)}, f32[8,64,128]{2,1,0:T(8,128)}, u32[]{:S(2)}) copy-start(f32[8,64,128]{2,1,0:T(8,128)} %param.11) | copy-start | bytes 786436
  3.5 0.9 %copy-start.5 = (f32[8,64,128]{2,1,0:T(8,128)S(1)}, f32[8,64,128]{2,1,0:T(8,128)}, u32[]{:S(2)}) copy-start(f32[8,64,128]{2,1,0:T(8,128)} %param.12) | copy-start | bytes 786436
  4.4 0.9 %copy-start.6 = (f32[8,64,128]{2,1,0:T(8,128)S(1)}, f32[8,64,128]{2,1,0:T(8,128)}, u32[]{:S(2)}) copy-start(f32[8,64,128]{2,1,0:T(8,128)} %param.15) | copy-start | bytes 786436
  5.4 0.9 %copy-start.7 = (s32[8,64,128]{2,1,0:T(8,128)S(1)}, s32[8,64,128]{2,1,0:T(8,128)}, u32[]{:S(2)}) copy-start(s32[8,64,128]{2,1,0:T(8,128)} %param.16) | copy-start | bytes 786436
  6.3 0.8 %copy-start.8 = (f32[64,128]{1,0:T(8,128)S(1)}, f32[64,128]{1,0:T(8,128)}, u32[]{:S(2)}) copy-start(f32[64,128]{1,0:T(8,128)} %refs_6_.5) | copy-start | bytes 98308
  7.1 0.8 %copy-start.9 = (f32[64,128]{1,0:T(8,128)S(1)}, f32[64,128]{1,0:T(8,128)}, u32[]{:S(2)}) copy-start(f32[64,128]{1,0:T(8,128)} %refs_7_.6) | copy-start | bytes 98308
  8.0 26.9 %collective-permute-start.1 = (f32[27,8,128]{2,1,0:T(8,128)S(1)}, f32[27,8,128]{2,1,0:T(8,128)S(1)}, u32[]{:S(2)}, u32[]{:S(2)}) collective-permute-start(f32[27,8,128]{2,1,0:T(8,128)S(1)} %get-tuple-element.20), channel_id=1, source_target_pairs={{16,32},{17,33},{18,34},{19,35},{20,36},{21,37},{22,38},{23,39},{2... | collective-permute-start | bytes 331784 | tf_op jit(solution)/shard_map/ppermute | solution.py:546
  14.5 20.3 %collective-permute-start = (f32[21,8,128]{2,1,0:T(8,128)S(1)}, f32[21,8,128]{2,1,0:T(8,128)S(1)}, u32[]{:S(2)}, u32[]{:S(2)}) collective-permute-start(f32[21,8,128]{2,1,0:T(8,128)S(1)} %get-tuple-element.19), channel_id=1, source_target_pairs={{0,16},{1,17},{2,18},{3,19},{4,20},{5,21},{6,22},{7,23},{8,24},{9,... | collective-permute-start | bytes 258056 | tf_op jit(solution)/shard_map/ppermute | solution.py:547
  14.6 23.0 %copy-start.3 = (f32[8,64,128]{2,1,0:T(8,128)S(1)}, f32[8,64,128]{2,1,0:T(8,128)}, u32[]{:S(2)}) copy-start(f32[8,64,128]{2,1,0:T(8,128)} %param.10) | copy-start | bytes 786436
  34.8 2.8 %copy-start.1 = (f32[8,64,128]{2,1,0:T(8,128)S(1)}, f32[8,64,128]{2,1,0:T(8,128)}, u32[]{:S(2)}) copy-start(f32[8,64,128]{2,1,0:T(8,128)} %param.9) | copy-start | bytes 786436
  35.1 10.2 %collective-permute-start.2 = (f32[18,8,128]{2,1,0:T(8,128)S(1)}, f32[18,8,128]{2,1,0:T(8,128)S(1)}, u32[]{:S(2)}, u32[]{:S(2)}) collective-permute-start(f32[18,8,128]{2,1,0:T(8,128)S(1)} %get-tuple-element.21), channel_id=1, source_target_pairs={{0,1},{1,0},{2,3},{3,2},{4,5},{5,4},{6,7},{7,6},{8,9},{9,8},{10,11... | collective-permute-start | bytes 221192 | tf_op jit(solution)/shard_map/ppermute | solution.py:558
  35.8 9.4 %collective-permute-start.3 = (f32[18,8,128]{2,1,0:T(8,128)S(1)}, f32[18,8,128]{2,1,0:T(8,128)S(1)}, u32[]{:S(2)}, u32[]{:S(2)}) collective-permute-start(f32[18,8,128]{2,1,0:T(8,128)S(1)} %get-tuple-element.22), channel_id=1, source_target_pairs={{0,15},{1,2},{2,1},{3,4},{4,3},{5,6},{6,5},{7,8},{8,7},{9,10},{10,... | collective-permute-start | bytes 221192 | tf_op jit(solution)/shard_map/ppermute | solution.py:557
where the time goes:
time: 55.6 us; the launch traced here: 55.1 us
  Pallas kernels  38 us (68%)
  starting transfers between devices  8.52 us (15%)
  local copies, waits for them, and re-layouts  7.22 us (13%)
  between operations  1.41 us (3%)
    pallas_call x5, Pallas kernels, call(): pl.pallas_call(kernel, out_shape=[jax.ShapeDtypeStruct(shape, F32) for sh...  38 us
    unnamed x20, local copies, waits for them, and re-layouts  7.22 us
    ppermute x1, starting transfers between devices, on_device(): got_b = lax.ppermute(rows_b, axes, pairs_b)  6.52 us
    ppermute x1, starting transfers between devices, on_device(): lon_b = lax.ppermute(cols_b, axes, pairs_b)  1.16 us
  transfers between devices with their start and end apart: 4, of which 0 were waited for; matrix products, arithmetic and copies ran while one was open for 0% of the time, Pallas kernels for 50%

commit v1 on v0

--- a/solution.py
+++ b/solution.py
@@ -25,7 +25,7 @@
 eos_cross = 0.0024341
 
 SIGNS = (1.0, 1.0, -1.0, -1.0)
-VMEM_LIMIT = 40 * 1024 * 1024
+MIB = 1024 * 1024
 
 
 def roll(x, shift):
@@ -94,7 +94,7 @@
     geo["inv"][row] = (0.5 * time_step) / (east0 * north0 * jnp.where(half0 > 0.0, half0, 1.0))
 
 
-def march(state, geo, bases, low, blocks, unroll):
+def march(state, geo, chains, unroll=None):
     terms = eos_terms()
 
     def north_face(row, speed):
@@ -102,48 +102,49 @@
         ahead = jnp.maximum(flow, 0.0) + geo["cond_n"][row]
         return ahead, flow - ahead
 
-    def first(base):
-        row = base + low
+    def begin(row):
         before = tuple(ref[row - 1] for ref in state)
         here = tuple(ref[row] for ref in state)
         return before + here + north_face(row - 1, before[3]) + (pressure_of(here[0], here[1], geo["half"][row], terms),)
 
-    def block(index, carries):
-        start = low + index * unroll
-        nexts = [[tuple(ref[base + start + u + 1] for ref in state) for u in range(unroll)] for base in bases]
-        after = []
-        stores = []
-        for base, ahead_rows, carry in zip(bases, nexts, carries):
-            before, here = carry[0:4], carry[4:8]
-            south_p, south_m, press = carry[8:]
+    def advance(row, carry):
+        before, here = carry[0:4], carry[4:8]
+        south_p, south_m, press = carry[8:]
+        north = tuple(ref[row + 1] for ref in state)
+        press_n = pressure_of(north[0], north[1], geo["half"][row + 1], terms)
+        north_p, north_m = north_face(row, here[3])
+        flow = geo["area_e"][row] * here[2]
+        east_p = jnp.maximum(flow, 0.0) + geo["cond_e"][row]
+        east_m = flow - east_p
+        west_p, west_m = roll(east_p, 1), roll(east_m, 1)
+        inv = geo["inv"][row]
+        keep = 1.0 - inv * ((east_p - west_m) + (north_p - south_m))
+        c_e, c_w, c_n, c_s = inv * east_m, inv * west_p, inv * north_m, inv * south_p
+        new = [
+            keep * c + (c_w * roll(c, 1) + c_s * s) - (c_e * roll(c, -1) + c_n * n)
+            for c, s, n in zip(here, before, north)
+        ]
+        new[2] = (new[2] + (press - roll(press, -1)) * geo["push_e"][row]) * geo["open_e"][row]
+        new[3] = (new[3] + (press - press_n) * geo["push_n"][row]) * geo["open_n"][row]
+        for ref, value in zip(state, new):
+            ref[row] = value
+        return here + north + (north_p, north_m, press_n)
+
+    carries = [begin(first) for first, _ in chains]
+    if unroll is None:
+        for u in range(max(count for _, count in chains)):
+            for index, (first, count) in enumerate(chains):
+                if u < count:
+                    carries[index] = advance(first + u, carries[index])
+    else:
+        ((first, count),) = chains
+
+        def block(index, carry):
             for u in range(unroll):
-                row = base + start + u
-                north = ahead_rows[u]
-                press_n = pressure_of(north[0], north[1], geo["half"][row + 1], terms)
-                north_p, north_m = north_face(row, here[3])
-                flow = geo["area_e"][row] * here[2]
-                east_p = jnp.maximum(flow, 0.0) + geo["cond_e"][row]
-                east_m = flow - east_p
-                west_p, west_m = roll(east_p, 1), roll(east_m, 1)
-                inv = geo["inv"][row]
-                keep = 1.0 - inv * ((east_p - west_m) + (north_p - south_m))
-                c_e, c_w, c_n, c_s = inv * east_m, inv * west_p, inv * north_m, inv * south_p
-                new = [
-                    keep * c + (c_w * roll(c, 1) + c_s * s) - (c_e * roll(c, -1) + c_n * n)
-                    for c, s, n in zip(here, before, north)
-                ]
-                new[2] = (new[2] + (press - roll(press, -1)) * geo["push_e"][row]) * geo["open_e"][row]
-                new[3] = (new[3] + (press - press_n) * geo["push_n"][row]) * geo["open_n"][row]
-                stores.append((row, new))
-                before, here = here, north
-                south_p, south_m, press = north_p, north_m, press_n
-            after.append(before + here + (south_p, south_m, press))
-        for row, new in stores:
-            for ref, value in zip(state, new):
-                ref[row] = value
-        return tuple(after)
-
-    lax.fori_loop(0, blocks, block, tuple(first(base) for base in bases))
+                carry = advance(first + index * unroll + u, carry)
+            return carry
+
+        lax.fori_loop(0, count // unroll, block, carries[0])
 
 
 GEO = ("half", "area_e", "cond_e", "open_e", "push_e", "area_n", "cond_n", "open_n", "push_n", "inv")
@@ -154,7 +155,7 @@
 
 
 def column_of(ref, row):
-    return ref[pl.ds(row, LEVELS, stride=ROWS), :]
+    return ref[pl.ds(row, LEVELS, stride=ref.shape[0] // LEVELS), :]
 
 
 def wide(ref, row):
@@ -168,22 +169,35 @@
 
 
 def rows_kernel(*refs):
-    ins, (out_a, out_b) = refs[:8], refs[8:]
-    even = lax.rem(lax.axis_index("lat"), 2) == 0
-    start_a = jnp.where(even, ROWS - HALO, 0)
-    start_b = jnp.where(even, 0, ROWS - HALO - 1)
+    ins, (out_a, out_b) = refs[:8], refs[8:10]
+    rims, sems = refs[10:18], refs[18]
+    copies = []
+    for f, (src, dst) in enumerate(zip(ins, rims)):
+        for side, row in ((0, 0), (1, ROWS - 8)):
+            if f < 6:
+                pair = src.at[:, pl.ds(row, 8), :], dst.at[side]
+            else:
+                pair = src.at[pl.ds(row, 8), :], dst.at[side]
+            copies.append(pltpu.make_async_copy(*pair, sems.at[f, side]))
+    for copy in copies:
+        copy.start()
     out_b[25] = jnp.ones((LEVELS, LANES), F32)
     out_b[26] = jnp.ones((LEVELS, LANES), F32)
-    for i in range(HALO):
-        for f, value in enumerate(own_row(ins, start_a + i)):
-            out_a[5 * i + f] = value
-        out_a[20, pl.ds(i, 1), :] = ins[6][pl.ds(start_a + i, 1), :]
-        out_a[20, pl.ds(HALO + i, 1), :] = ins[7][pl.ds(start_a + i, 1), :]
-    for i in range(HALO + 1):
-        for f, value in enumerate(own_row(ins, start_b + i)):
-            out_b[5 * i + f] = value
-        out_b[25, pl.ds(i, 1), :] = ins[6][pl.ds(start_b + i, 1), :]
-        out_b[26, pl.ds(i, 1), :] = ins[7][pl.ds(start_b + i, 1), :]
+    for copy in copies:
+        copy.wait()
+    even = lax.rem(lax.axis_index("lat"), 2) == 0
+    side_a = jnp.where(even, 1, 0)
+    row_a = jnp.where(even, HALO, 0)
+    side_b = jnp.where(even, 0, 1)
+    row_b = jnp.where(even, 0, HALO - 1)
+    for out, side, row, count, flat in ((out_a, side_a, row_a, HALO, 0), (out_b, side_b, row_b, HALO + 1, 1)):
+        cut = [ref.at[side].reshape(LEVELS * 8, LANES) for ref in rims[:6]]
+        for i in range(count):
+            for f, value in enumerate(own_row(cut, row + i)):
+                out[5 * i + f] = value
+            for f in range(2):
+                place = (20, HALO * f + i) if flat == 0 else (25 + f, i)
+                out[place[0], pl.ds(place[1], 1), :] = rims[6 + f][side, pl.ds(row + i, 1), :]
 
 
 def halo_rows(got_a, got_b):
@@ -219,18 +233,29 @@
 
 def interior_kernel(*refs):
     ins = refs[:8]
-    state_out, own, msgs = refs[8:11]
+    state_out, own, msgs, rims = refs[8:12]
     state = [state_out.at[f] for f in range(4)]
-    geo = dict(zip(GEO, refs[11:]))
+    geo = dict(zip(GEO, refs[12:22]))
+    blank = jnp.zeros((LEVELS, LANES), F32)
+    for ref in state + [geo["half"]]:
+        ref[0] = blank
+        ref[ROWS + 1] = blank
 
     def take(row, carry):
         values = own_row(ins, row)
         for ref, value in zip(state, values):
-            ref[row] = value
-        geo["half"][row] = values[4]
+            ref[row + 1] = value
+        geo["half"][row + 1] = values[4]
         return carry
 
-    lax.fori_loop(0, ROWS, take, 0)
+    lax.fori_loop(0, ROWS, take, 0, unroll=8)
+    for i in range(8):
+        for place, row in ((i, i), (8 + i, ROWS - 8 + i)):
+            for f in range(4):
+                rims[f, place] = state[f][row + 1]
+            rims[4, place] = geo["half"][row + 1]
+            rims[5, place] = wide(ins[6], row)
+            rims[6, place] = wide(ins[7], row)
 
     lane = lanes()
     part = (lane // HALO) % (GROUP // HALO)
@@ -242,9 +267,9 @@
             for q in range(8):
                 row = jnp.clip(BLOCK * q + g - HALO, 0, ROWS - 1)
                 if f < 4:
-                    value = state[f][row]
+                    value = state[f][row + 1]
                 elif f == 4:
-                    value = geo["half"][row]
+                    value = geo["half"][row + 1]
                 else:
                     value = wide(ins[f + 1], row)
                 here = (lane // GROUP) == q
@@ -266,13 +291,14 @@
     lax.fori_loop(0, BLOCK, pack, 0)
 
     def shape(row, carry):
-        geometry_row(geo, row, wide(ins[6], row), wide(ins[7], row), wide(ins[6], row + 1), wide(ins[7], row + 1))
+        geometry_row(geo, row + 1, wide(ins[6], row), wide(ins[7], row), wide(ins[6], row + 1), wide(ins[7], row + 1))
         return carry
 
-    lax.fori_loop(0, ROWS - 1, shape, 0)
+    lax.fori_loop(0, ROWS - 1, shape, 0, unroll=7)
 
     def step(s, carry):
-        march(state, geo, (0,), s, 32 - s, 2)
+        last = s == NSTEP
+        march(state, geo, ((jnp.where(last, 1 + HALO, 1), jnp.where(last, ROWS - 2 * HALO, ROWS)),), 8)
         return carry
 
     lax.fori_loop(1, NSTEP + 1, step, 0)
@@ -313,56 +339,42 @@
 
 
 def rows_strip_kernel(*refs):
-    ins = refs[:8]
-    got_a, got_b, hinge, out = refs[8:12]
-    state = refs[12:16]
-    east_w, north_w = refs[16:18]
-    geo = dict(zip(GEO, refs[18:]))
+    rims, got_a, got_b, hinge, out = refs[:5]
+    state = refs[5:9]
+    east_w, north_w = refs[9:11]
+    geo = dict(zip(GEO, refs[11:]))
     top = lax.axis_index("lat") == lax.axis_size("lat") - 1
     pivot = hinge[0]
     south, north, fold = halo_rows(got_a, got_b)
     fields = list(state) + [geo["half"], east_w, north_w]
-    for i in range(HALO):
-        for f, ref in enumerate(fields):
+    for f, ref in enumerate(fields):
+        for i in range(HALO):
             ref[SOUTH + i] = south(i, f)
             ref[NORTH + 8 + i] = north(i, f)
-    for i in range(8):
-        for base, row in ((SOUTH + HALO, i), (NORTH, ROWS - 8 + i)):
-            for ref, value in zip(fields, own_row(ins, row) + (wide(ins[6], row), wide(ins[7], row))):
-                ref[base + i] = value
+            ref[FOLD + i] = fold(i, f)
+        ref[FOLD + HALO] = fold(HALO, f)
+        for i in range(8):
+            ref[SOUTH + HALO + i] = rims[f, i]
+            ref[NORTH + i] = rims[f, 8 + i]
 
     def refold(ref, sign):
         ghost = sign * mirrored(ref[FOLD + 4 - pivot], LANES)
         ref[FOLD + 5] = sign * mirrored(ref[NORTH + 7 - pivot], LANES)
-        ref[NORTH + 8] = ghost
-
-    def shape(row, carry):
+        ref[NORTH + 8] = jnp.where(top, ghost, ref[NORTH + 8])
+
+    for ref in fields[4:]:
+        refold(ref, 1.0)
+    for row in (*range(SOUTH, SOUTH + 11), *range(NORTH, NORTH + 11), *range(FOLD, FOLD + 5)):
         geometry_row(geo, row, east_w[row], north_w[row], east_w[row + 1], north_w[row + 1])
-        return carry
-
-    @pl.when(top)
-    def _():
-        for i in range(HALO + 1):
-            for f, ref in enumerate(fields):
-                ref[FOLD + i] = fold(i, f)
-        for ref in fields[4:]:
-            refold(ref, 1.0)
-        lax.fori_loop(FOLD, FOLD + 5, shape, 0)
-
-    lax.fori_loop(SOUTH, SOUTH + 11, shape, 0)
-    lax.fori_loop(NORTH, NORTH + 11, shape, 0)
-
-    def step(s, carry):
-        @pl.when(top)
-        def _():
-            for ref, sign in zip(state, SIGNS):
-                refold(ref, sign)
-            march(state, geo, (FOLD,), s, 5 - s, 1)
-
-        march(state, geo, (SOUTH, NORTH), s, 6 - s, 2)
-        return carry
-
-    lax.fori_loop(1, NSTEP + 1, step, 0)
+
+    for s in range(1, NSTEP + 1):
+        for ref, sign in zip(state, SIGNS):
+            refold(ref, sign)
+        chains = [(SOUTH + s, 12 - 2 * s), (NORTH + s, 12 - 2 * s)]
+        if s < NSTEP:
+            chains.append((FOLD + s, 5 - s))
+        march(state, geo, chains)
+
     for f, ref in enumerate(state):
         for i in range(HALO):
             out[f, i] = ref[SOUTH + HALO + i]
@@ -421,52 +433,34 @@
         from_e, from_w = ref[EAST + 5 - pivot], ref[WEST + 5 - pivot]
         back = jnp.where(lane < GROUP, roll(from_e, GROUP), roll(from_w, 2 * GROUP))
         ref[FOLDS + 5] = sign * mirrored(back, GROUP)
-        here = lane >= 7 * GROUP
+        here = (lane >= 7 * GROUP) & top
         ref[WEST + 6] = jnp.where(here, roll(ghost, 6 * GROUP), ref[WEST + 6])
         ref[EAST + 6] = jnp.where(here, roll(ghost, 7 * GROUP), ref[EAST + 6])
 
-    def shape(row, carry):
+    for i in range(HALO + 1):
+        for f, ref in enumerate(fields):
+            value = fold(i, f)
+            value = jnp.where(lane < GROUP, roll(value, HALO), roll(value, 28))
+            if i > 0:
+                slot = HALO + i
+                corner = 7 * GROUP + HALO * (f % 4)
+                value = jnp.where(lane < HALO, roll(message(1, f, slot), -corner), value)
+                other = roll(message(0, f, slot), 28 - corner)
+                value = jnp.where((lane >= 28) & (lane < 32), other, value)
+            if f > 4:
+                value = jnp.where(value > 0.0, value, 1.0)
+            ref[FOLDS + i] = value
+    for ref in fields[4:]:
+        refold(ref, 1.0)
+        rewrap(ref)
+    for row in (*range(WEST, WEST + 10), *range(EAST, EAST + 10), *range(FOLDS, FOLDS + 5)):
         geometry_row(geo, row, east_w[row], north_w[row], east_w[row + 1], north_w[row + 1])
-        return carry
-
-    @pl.when(top)
-    def _():
-        for i in range(HALO + 1):
-            for f, ref in enumerate(fields):
-                value = fold(i, f)
-                value = jnp.where(lane < GROUP, roll(value, HALO), roll(value, 28))
-                if i > 0:
-                    slot = HALO + i
-                    corner = 7 * GROUP + HALO * (f % 4)
-                    value = jnp.where(lane < HALO, roll(message(1, f, slot), -corner), value)
-                    other = roll(message(0, f, slot), 28 - corner)
-                    value = jnp.where((lane >= 28) & (lane < 32), other, value)
-                if f > 4:
-                    value = jnp.where(value > 0.0, value, 1.0)
-                ref[FOLDS + i] = value
-        for ref in fields[4:]:
-            refold(ref, 1.0)
-
-    for ref in fields[4:]:
-        rewrap(ref)
-
-    lax.fori_loop(WEST, WEST + 10, shape, 0)
-    lax.fori_loop(EAST, EAST + 10, shape, 0)
-
-    @pl.when(top)
-    def _():
-        lax.fori_loop(FOLDS, FOLDS + 5, shape, 0)
 
     def step(s, carry):
-        @pl.when(top)
-        def _():
-            for ref, sign in zip(state, SIGNS):
-                refold(ref, sign)
-            march(state, geo, (FOLDS,), s, 5 - s, 1)
-
-        for ref in state:
+        for ref, sign in zip(state, SIGNS):
+            refold(ref, sign)
             rewrap(ref)
-        march(state, geo, (WEST, EAST), 1, 3, 3)
+        march(state, geo, ((WEST + 1, BLOCK), (EAST + 1, BLOCK), (FOLDS + 1, 4)))
         return carry
 
     lax.fori_loop(1, NSTEP + 1, step, 0)
@@ -488,20 +482,20 @@
     for i in range(HALO):
         emit(i, [strips[f, i] for f in range(4)], 0, HALO + i)
         emit(ROWS - HALO + i, [strips[f, HALO + i] for f in range(4)], 7, 1 + i)
-    emit(HALO, [inner[f, HALO] for f in range(4)], 0, 8)
-    emit(ROWS - HALO - 1, [inner[f, ROWS - HALO - 1] for f in range(4)], 7, 0)
+    emit(HALO, [inner[f, HALO + 1] for f in range(4)], 0, 8)
+    emit(ROWS - HALO - 1, [inner[f, ROWS - HALO] for f in range(4)], 7, 0)
 
     def merge(g, carry):
         for q in range(1, 7):
             row = BLOCK * q + g - HALO
-            emit(row, [inner[f, row] for f in range(4)], q, g)
+            emit(row, [inner[f, row + 1] for f in range(4)], q, g)
         return carry
 
     lax.fori_loop(0, BLOCK, merge, 0)
 
 
-def call(kernel, ins, outs, scratch=(), smem_last=False, flops=0):
-    specs = [pl.BlockSpec(memory_space=pltpu.VMEM) for _ in ins]
+def call(kernel, ins, outs, scratch=(), smem_last=False, far=False, flops=0, limit=40):
+    specs = [pl.BlockSpec(memory_space=pltpu.HBM if far else pltpu.VMEM) for _ in ins]
     if smem_last:
         specs[-1] = pl.BlockSpec(memory_space=pltpu.SMEM)
     return pl.pallas_call(
@@ -510,7 +504,7 @@
         in_specs=specs,
         out_specs=[pl.BlockSpec(memory_space=pltpu.VMEM) for _ in outs],
         scratch_shapes=list(scratch),
-        compiler_params=pltpu.CompilerParams(vmem_limit_bytes=VMEM_LIMIT),
+        compiler_params=pltpu.CompilerParams(vmem_limit_bytes=limit * MIB),
         cost_estimate=pl.CostEstimate(flops=flops, bytes_accessed=2_000_000, transcendentals=0),
     )(*ins)
 
@@ -535,22 +529,33 @@
 def on_device(*args):
     lat, lon = lax.axis_size("lat"), lax.axis_size("lon")
     axes = ("lat", "lon")
-    flat = [x.reshape(LEVELS * ROWS, LANES) for x in (*args[:4], args[6], args[7])]
-    ins = flat + [args[4], args[5]]
     hinge = args[8]
     tile = (LEVELS, LANES)
+    fields = [*args[:4], args[6], args[7], args[4], args[5]]
+    flat = [x.reshape(LEVELS * ROWS, LANES) for x in fields[:6]] + fields[6:]
+    kinds = [F32] * 5 + [jnp.int32] + [F32] * 2
     state_scratch = lambda rows: [pltpu.VMEM((rows,) + tile, F32) for _ in range(6)]
 
-    rows_a, rows_b = call(rows_kernel, ins, [(21,) + tile, (27,) + tile])
+    rows_a, rows_b = call(
+        rows_kernel,
+        fields,
+        [(21,) + tile, (27,) + tile],
+        [pltpu.VMEM((2, LEVELS) + tile, kind) for kind in kinds[:6]]
+        + [pltpu.VMEM((2,) + tile, F32)] * 2
+        + [pltpu.SemaphoreType.DMA((8, 2))],
+        far=True,
+        limit=54,
+    )
     pairs_a, pairs_b = lat_pairs(lat, lon)
     got_b = lax.ppermute(rows_b, axes, pairs_b)
     got_a = lax.ppermute(rows_a, axes, pairs_a)
-    inner, own, msgs = call(
+    inner, own, msgs, rims = call(
         interior_kernel,
-        ins,
-        [(4, ROWS) + tile, (2, 7, BLOCK) + tile, (2, 2 * BLOCK) + tile],
-        geo_scratch(ROWS),
+        flat,
+        [(4, ROWS + 2) + tile, (2, 7, BLOCK) + tile, (2, 2 * BLOCK) + tile, (7, 16) + tile],
+        geo_scratch(ROWS + 2),
         flops=40_000_000,
+        limit=50,
     )
     cols_a, cols_b = call(columns_kernel, [msgs, got_a, got_b], [(2 * BLOCK,) + tile] * 2)
     pairs_a, pairs_b = lon_pairs(lat, lon)
@@ -558,7 +563,7 @@
     lon_a = lax.ppermute(cols_a, axes, pairs_a)
     (strips,) = call(
         rows_strip_kernel,
-        ins + [got_a, got_b, hinge],
+        [rims, got_a, got_b, hinge],
         [(4, 2 * HALO) + tile],
         state_scratch(NS_ROWS) + geo_scratch(NS_ROWS),
         smem_last=True,

time: 55.6 us -> 33.9 us (0.61)
  the two profiles are of different devices: /device:TPU:56 before, /device:TPU:48 now
where the time goes in v1:
time: 33.9 us; the launch traced here: 33.7 us
  Pallas kernels  20 us (59%)
  starting transfers between devices  8.65 us (26%)
  waiting for transfers between devices  3.62 us (11%)
  between operations  1.44 us (4%)
    pallas_call x5, Pallas kernels, call(): pl.pallas_call(kernel, out_shape=[jax.ShapeDtypeStruct(shape, F32) for sh...  20 us
    ppermute x1, starting transfers between devices, on_device(): got_a = lax.ppermute(rows_a, axes, pairs_a)  5.52 us
    ppermute x1, waiting for transfers between devices, on_device(): lon_b = lax.ppermute(cols_b, axes, pairs_b)  3.61 us
    ppermute x1, starting transfers between devices, on_device(): got_b = lax.ppermute(rows_b, axes, pairs_b)  2.36 us
  transfers between devices with their start and end apart: 4, of which 1 were waited for; matrix products, arithmetic and copies ran while one was open for 0% of the time, Pallas kernels for 36%

profile of v1, /device:TPU:48, one launch (start us, length us, event | category | flops | bytes accessed | tf_op | source)
XLA Modules:
  0.0 33.7 jit_solution(4660804977751081869)
XLA Ops:
  0.6 0.0 copy-start.5
  0.6 0.0 copy-start.4
  0.7 0.0 copy-start.7
  0.7 0.0 copy-start.6
  0.7 0.0 copy-start.3
  0.7 0.0 copy-start.2
  0.7 0.0 copy-start.1
  0.7 0.0 copy-start
  0.7 1.9 %shard_map.129 = (f32[21,8,128]{2,1,0:T(8,128)}, f32[27,8,128]{2,1,0:T(8,128)}) custom-call(f32[8,64,128]{2,1,0:T(8,128)} %refs_0_.1, f32[8,64,128]{2,1,0:T(8,128)} %refs_1_.1, f32[8,64,128]{2,1,0:T(8,128)} %refs_2_.1, f32[8,64,128]{2,1,0:T(8,128)} %refs_3_.2, f32[8,64,128]{2,1,0:T(8,128)} %refs_4_.1, s32[8,64,128]{2,1,0:T(8,128)} %refs_5_.1, ...), custom_call_target="tpu_custom_call" | custom-call | bytes 2000000 | tf_op jit(solution)/shard_map/pallas_call | solution.py:501
  2.6 2.4 %collective-permute-start.1 = (f32[27,8,128]{2,1,0:T(8,128)}, f32[27,8,128]{2,1,0:T(8,128)S(1)}, u32[]{:S(2)}, u32[]{:S(2)}) collective-permute-start(f32[27,8,128]{2,1,0:T(8,128)} %get-tuple-element.21), channel_id=1, source_target_pairs={{16,32},{17,33},{18,34},{19,35},{20,36},{21,37},{22,38},{23,39},{2... | collective-permute-start | bytes 331784 | tf_op jit(solution)/shard_map/ppermute | solution.py:550
  5.0 5.5 %collective-permute-start = (f32[21,8,128]{2,1,0:T(8,128)}, f32[21,8,128]{2,1,0:T(8,128)S(1)}, u32[]{:S(2)}, u32[]{:S(2)}) collective-permute-start(f32[21,8,128]{2,1,0:T(8,128)} %get-tuple-element.20), channel_id=1, source_target_pairs={{0,16},{1,17},{2,18},{3,19},{4,20},{5,21},{6,22},{7,23},{8,24},{9,... | collective-permute-start | bytes 258056 | tf_op jit(solution)/shard_map/ppermute | solution.py:551
  10.5 0.0 copy-done.5
  10.5 0.0 copy-done.4
  10.5 0.0 copy-done.7
  10.5 0.0 copy-done.6
  10.5 0.0 copy-done.3
  10.5 0.0 copy-done.2
  10.5 0.0 copy-done.1
  10.6 0.0 copy-done
  10.6 9.3 %shard_map.128 = (f32[4,66,8,128]{3,2,1,0:T(8,128)S(1)}, f32[2,7,9,8,128]{4,3,2,1,0:T(8,128)S(1)}, f32[2,18,8,128]{3,2,1,0:T(8,128)S(1)}, f32[7,16,8,128]{3,2,1,0:T(8,128)S(1)}) custom-call(f32[512,128]{1,0:T(8,128)S(1)} %bitcast.11, f32[512,128]{1,0:T(8,128)S(1)} %bitcast.12, f32[512,128]{1,0:T(8,128)S(1)} %bitcast.13, f32[512,128]{1,0:T(8,128)S(1)} %bitcast.14, ...), custom_call_target="tpu_custom_call" | custom-call | flops 40000000 | bytes 2000000 | tf_op jit(solution)/shard_map/pallas_call | solution.py:501
  19.9 0.0 collective-permute-done.got_a.refs_1_.refs_3_
  19.9 0.0 collective-permute-done.1.got_b.refs_2_.refs_4_
  19.9 0.2 shard_map.130
  20.1 0.5 %collective-permute-start.2 = (f32[18,8,128]{2,1,0:T(8,128)S(1)}, f32[18,8,128]{2,1,0:T(8,128)S(1)}, u32[]{:S(2)}, u32[]{:S(2)}) collective-permute-start(f32[18,8,128]{2,1,0:T(8,128)S(1)} %get-tuple-element.22), channel_id=1, source_target_pairs={{0,1},{1,0},{2,3},{3,2},{4,5},{5,4},{6,7},{7,6},{8,9},{9,8},{10,11... | collective-permute-start | bytes 221192 | tf_op jit(solution)/shard_map/ppermute | solution.py:563
  20.6 0.3 collective-permute-start.3
  21.6 2.8 %shard_map.131.refs_6_ = f32[4,8,8,128]{3,2,1,0:T(8,128)S(1)} custom-call(f32[7,16,8,128]{3,2,1,0:T(8,128)S(1)} %get-tuple-element.25.refs_0_, f32[21,8,128]{2,1,0:T(8,128)S(1)} %collective-permute-done.got_a.refs_1_.refs_3_, f32[27,8,128]{2,1,0:T(8,128)S(1)} %collective-permute-done.1.got_b.refs_2_.refs_4_, s32[1]{0:T(128)S(6)} %copy.14.refs_3_.refs_7_), custom_call_target="tpu_custom_call" | custom-call | flops 10000000 | bytes 2000000 | tf_op jit(solution)/shard_map/pallas_call | solution.py:501
  24.4 0.0 collective-permute-done.2.refs_1_
  24.4 3.6 %collective-permute-done.3.refs_2_ = f32[18,8,128]{2,1,0:T(8,128)S(1)} collective-permute-done((f32[18,8,128]{2,1,0:T(8,128)S(1)}, f32[18,8,128]{2,1,0:T(8,128)S(1)}, u32[]{:S(2)}, u32[]{:S(2)}) %collective-permute-start.3) | collective-permute-done | bytes 73760 | tf_op jit(solution)/shard_map/ppermute | solution.py:562
  28.0 5.7 %shard_map.132 = (f32[512,128]{1,0:T(8,128)}, f32[512,128]{1,0:T(8,128)}, f32[512,128]{1,0:T(8,128)}, f32[512,128]{1,0:T(8,128)}, f32[512,128]{1,0:T(8,128)}) custom-call(f32[2,7,9,8,128]{4,3,2,1,0:T(8,128)S(1)} %get-tuple-element.18.refs_0_, f32[18,8,128]{2,1,0:T(8,128)S(1)} %collective-permute-done.2.refs_1_, ...), custom_call_target="tpu_custom_call" | custom-call | flops 10000000 | bytes 2000000 | tf_op jit(solution)/shard_map/pallas_call | solution.py:501
Async XLA Ops:
  0.6 9.9 %copy-start.5 = (s32[8,64,128]{2,1,0:T(8,128)S(1)}, s32[8,64,128]{2,1,0:T(8,128)}, u32[]{:S(2)}) copy-start(s32[8,64,128]{2,1,0:T(8,128)} %refs_5_.1) | copy-start | bytes 786436
  0.6 9.9 %copy-start.4 = (f32[8,64,128]{2,1,0:T(8,128)S(1)}, f32[8,64,128]{2,1,0:T(8,128)}, u32[]{:S(2)}) copy-start(f32[8,64,128]{2,1,0:T(8,128)} %refs_4_.1) | copy-start | bytes 786436
  0.7 9.9 %copy-start.7 = (f32[64,128]{1,0:T(8,128)S(1)}, f32[64,128]{1,0:T(8,128)}, u32[]{:S(2)}) copy-start(f32[64,128]{1,0:T(8,128)} %refs_7_.4) | copy-start | bytes 98308
  0.7 9.9 %copy-start.6 = (f32[64,128]{1,0:T(8,128)S(1)}, f32[64,128]{1,0:T(8,128)}, u32[]{:S(2)}) copy-start(f32[64,128]{1,0:T(8,128)} %refs_6_.3) | copy-start | bytes 98308
  0.7 9.9 %copy-start.3 = (f32[8,64,128]{2,1,0:T(8,128)S(1)}, f32[8,64,128]{2,1,0:T(8,128)}, u32[]{:S(2)}) copy-start(f32[8,64,128]{2,1,0:T(8,128)} %refs_3_.2) | copy-start | bytes 786436
  0.7 9.9 %copy-start.2 = (f32[8,64,128]{2,1,0:T(8,128)S(1)}, f32[8,64,128]{2,1,0:T(8,128)}, u32[]{:S(2)}) copy-start(f32[8,64,128]{2,1,0:T(8,128)} %refs_2_.1) | copy-start | bytes 786436
  0.7 9.9 %copy-start.1 = (f32[8,64,128]{2,1,0:T(8,128)S(1)}, f32[8,64,128]{2,1,0:T(8,128)}, u32[]{:S(2)}) copy-start(f32[8,64,128]{2,1,0:T(8,128)} %refs_1_.1) | copy-start | bytes 786436
  0.7 9.9 %copy-start = (f32[8,64,128]{2,1,0:T(8,128)S(1)}, f32[8,64,128]{2,1,0:T(8,128)}, u32[]{:S(2)}) copy-start(f32[8,64,128]{2,1,0:T(8,128)} %refs_0_.1) | copy-start | bytes 786436
  2.6 17.3 %collective-permute-start.1 = (f32[27,8,128]{2,1,0:T(8,128)}, f32[27,8,128]{2,1,0:T(8,128)S(1)}, u32[]{:S(2)}, u32[]{:S(2)}) collective-permute-start(f32[27,8,128]{2,1,0:T(8,128)} %get-tuple-element.21), channel_id=1, source_target_pairs={{16,32},{17,33},{18,34},{19,35},{20,36},{21,37},{22,38},{23,39},{2... | collective-permute-start | bytes 331784 | tf_op jit(solution)/shard_map/ppermute | solution.py:550
  5.0 14.9 %collective-permute-start = (f32[21,8,128]{2,1,0:T(8,128)}, f32[21,8,128]{2,1,0:T(8,128)S(1)}, u32[]{:S(2)}, u32[]{:S(2)}) collective-permute-start(f32[21,8,128]{2,1,0:T(8,128)} %get-tuple-element.20), channel_id=1, source_target_pairs={{0,16},{1,17},{2,18},{3,19},{4,20},{5,21},{6,22},{7,23},{8,24},{9,... | collective-permute-start | bytes 258056 | tf_op jit(solution)/shard_map/ppermute | solution.py:551
  20.1 4.3 %collective-permute-start.2 = (f32[18,8,128]{2,1,0:T(8,128)S(1)}, f32[18,8,128]{2,1,0:T(8,128)S(1)}, u32[]{:S(2)}, u32[]{:S(2)}) collective-permute-start(f32[18,8,128]{2,1,0:T(8,128)S(1)} %get-tuple-element.22), channel_id=1, source_target_pairs={{0,1},{1,0},{2,3},{3,2},{4,5},{5,4},{6,7},{7,6},{8,9},{9,8},{10,11... | collective-permute-start | bytes 221192 | tf_op jit(solution)/shard_map/ppermute | solution.py:563
  20.6 7.4 %collective-permute-start.3 = (f32[18,8,128]{2,1,0:T(8,128)S(1)}, f32[18,8,128]{2,1,0:T(8,128)S(1)}, u32[]{:S(2)}, u32[]{:S(2)}) collective-permute-start(f32[18,8,128]{2,1,0:T(8,128)S(1)} %get-tuple-element.23), channel_id=1, source_target_pairs={{0,15},{1,2},{2,1},{3,4},{4,3},{5,6},{6,5},{7,8},{8,7},{9,10},{10,... | collective-permute-start | bytes 221192 | tf_op jit(solution)/shard_map/ppermute | solution.py:562

commit v2 on v1

--- a/solution.py
+++ b/solution.py
@@ -94,7 +94,7 @@
     geo["inv"][row] = (0.5 * time_step) / (east0 * north0 * jnp.where(half0 > 0.0, half0, 1.0))
 
 
-def march(state, geo, chains, unroll=None):
+def march(state, geo, chains):
     terms = eos_terms()
 
     def north_face(row, speed):
@@ -131,20 +131,10 @@
         return here + north + (north_p, north_m, press_n)
 
     carries = [begin(first) for first, _ in chains]
-    if unroll is None:
-        for u in range(max(count for _, count in chains)):
-            for index, (first, count) in enumerate(chains):
-                if u < count:
-                    carries[index] = advance(first + u, carries[index])
-    else:
-        ((first, count),) = chains
-
-        def block(index, carry):
-            for u in range(unroll):
-                carry = advance(first + index * unroll + u, carry)
-            return carry
-
-        lax.fori_loop(0, count // unroll, block, carries[0])
+    for u in range(max(count for _, count in chains)):
+        for index, (first, count) in enumerate(chains):
+            if u < count:
+                carries[index] = advance(first + u, carries[index])
 
 
 GEO = ("half", "area_e", "cond_e", "open_e", "push_e", "area_n", "cond_n", "open_n", "push_n", "inv")
@@ -288,7 +278,7 @@
                 msgs[side, BLOCK * half + g] = message
         return carry
 
-    lax.fori_loop(0, BLOCK, pack, 0)
+    lax.fori_loop(0, BLOCK, pack, 0, unroll=3)
 
     def shape(row, carry):
         geometry_row(geo, row + 1, wide(ins[6], row), wide(ins[7], row), wide(ins[6], row + 1), wide(ins[7], row + 1))
@@ -297,8 +287,7 @@
     lax.fori_loop(0, ROWS - 1, shape, 0, unroll=7)
 
     def step(s, carry):
-        last = s == NSTEP
-        march(state, geo, ((jnp.where(last, 1 + HALO, 1), jnp.where(last, ROWS - 2 * HALO, ROWS)),), 8)
+        march(state, geo, ((2, ROWS - 2),))
         return carry
 
     lax.fori_loop(1, NSTEP + 1, step, 0)
@@ -389,10 +378,11 @@
     outs = refs[8:13]
     state = refs[13:17]
     east_w, north_w = refs[17:19]
-    geo = dict(zip(GEO, refs[19:]))
+    geo = dict(zip(GEO, refs[19:29]))
+    stage, sems = refs[29:34], refs[34]
     even = lax.rem(lax.axis_index("lon"), 2) == 0
     top = lax.axis_index("lat") == lax.axis_size("lat") - 1
-    pivot = hinge[0]
+    below = hinge[0] == 1
     south, north, fold = halo_rows(got_a, got_b)
     fields = list(state) + [geo["half"], east_w, north_w]
     lane = lanes()
@@ -429,8 +419,9 @@
             ref[base + 10] = roll(ref[base + 1], -GROUP)
 
     def refold(ref, sign):
-        ghost = sign * mirrored(ref[FOLDS + 4 - pivot], GROUP)
-        from_e, from_w = ref[EAST + 5 - pivot], ref[WEST + 5 - pivot]
+        ghost = sign * mirrored(jnp.where(below, ref[FOLDS + 3], ref[FOLDS + 4]), GROUP)
+        from_e = jnp.where(below, ref[EAST + 4], ref[EAST + 5])
+        from_w = jnp.where(below, ref[WEST + 4], ref[WEST + 5])
         back = jnp.where(lane < GROUP, roll(from_e, GROUP), roll(from_w, 2 * GROUP))
         ref[FOLDS + 5] = sign * mirrored(back, GROUP)
         here = (lane >= 7 * GROUP) & top
@@ -471,30 +462,31 @@
     rim = (lane < HALO) | (lane >= LANES - HALO)
     terms = eos_terms()
 
-    def emit(row, bases, q, g):
+    copies = []
+    for row in range(ROWS):
+        q, g = divmod(row + HALO, BLOCK)
+        if HALO <= row < ROWS - HALO:
+            bases = [inner[f, row + 1] for f in range(4)]
+        else:
+            place = row if row < HALO else row - (ROWS - 2 * HALO)
+            bases = [strips[f, place] for f in range(4)]
         new = [
             jnp.where(rim, roll(ref[WEST + 1 + g], -(GROUP * q + HALO)), base) for ref, base in zip(state, bases)
         ]
         new.append(density_of(new[0], new[1], terms))
-        for ref, value in zip(outs, new):
-            ref[pl.ds(row, LEVELS, stride=ROWS), :] = value
-
-    for i in range(HALO):
-        emit(i, [strips[f, i] for f in range(4)], 0, HALO + i)
-        emit(ROWS - HALO + i, [strips[f, HALO + i] for f in range(4)], 7, 1 + i)
-    emit(HALO, [inner[f, HALO + 1] for f in range(4)], 0, 8)
-    emit(ROWS - HALO - 1, [inner[f, ROWS - HALO] for f in range(4)], 7, 0)
-
-    def merge(g, carry):
-        for q in range(1, 7):
-            row = BLOCK * q + g - HALO
-            emit(row, [inner[f, row + 1] for f in range(4)], q, g)
-        return carry
-
-    lax.fori_loop(0, BLOCK, merge, 0)
-
-
-def call(kernel, ins, outs, scratch=(), smem_last=False, far=False, flops=0, limit=40):
+        for ref, value in zip(stage, new):
+            ref.reshape(LEVELS * ROWS, LANES)[pl.ds(row, LEVELS, stride=ROWS), :] = value
+        if row % 8 == 7:
+            rows = pl.ds(row - 7, 8)
+            for f in range(5):
+                copy = pltpu.make_async_copy(stage[f].at[:, rows, :], outs[f].at[:, rows, :], sems.at[f, row // 8])
+                copy.start()
+                copies.append(copy)
+    for copy in copies:
+        copy.wait()
+
+
+def call(kernel, ins, outs, scratch=(), smem_last=False, far=False, out_far=False, flops=0, limit=40):
     specs = [pl.BlockSpec(memory_space=pltpu.HBM if far else pltpu.VMEM) for _ in ins]
     if smem_last:
         specs[-1] = pl.BlockSpec(memory_space=pltpu.SMEM)
@@ -502,7 +494,7 @@
         kernel,
         out_shape=[jax.ShapeDtypeStruct(shape, F32) for shape in outs],
         in_specs=specs,
-        out_specs=[pl.BlockSpec(memory_space=pltpu.VMEM) for _ in outs],
+        out_specs=[pl.BlockSpec(memory_space=pltpu.HBM if out_far else pltpu.VMEM) for _ in outs],
         scratch_shapes=list(scratch),
         compiler_params=pltpu.CompilerParams(vmem_limit_bytes=limit * MIB),
         cost_estimate=pl.CostEstimate(flops=flops, bytes_accessed=2_000_000, transcendentals=0),
@@ -572,12 +564,16 @@
     outs = call(
         columns_strip_kernel,
         [own, lon_a, lon_b, got_a, got_b, inner, strips, hinge],
-        [(LEVELS * ROWS, LANES)] * 5,
-        state_scratch(WE_ROWS) + geo_scratch(WE_ROWS),
+        [(LEVELS, ROWS, LANES)] * 5,
+        state_scratch(WE_ROWS)
+        + geo_scratch(WE_ROWS)
+        + [pltpu.VMEM((LEVELS, ROWS, LANES), F32)] * 5
+        + [pltpu.SemaphoreType.DMA((5, 8))],
+        out_far=True,
         smem_last=True,
         flops=10_000_000,
     )
-    return tuple(x.reshape(LEVELS, ROWS, LANES) for x in outs)
+    return tuple(outs)
 
 
 def solution(mesh):

time: 33.9 us -> 30.8 us (0.909)
  Pallas kernels: 20 us -> 17 us
    pallas_call x5, Pallas kernels: 20 us -> 17 us  [call(): pl.pallas_call(kernel, out_shape=[jax.ShapeDtypeStruct(shape, F32) for sh...]
  transfers between devices with their start and end apart: 4 -> 4, of which waited for: 1 -> 1; matrix products, arithmetic and copies ran while one was open for 0% -> 0% of each run, Pallas kernels for 36% -> 32%
where the time goes in v2:
time: 30.8 us; the launch traced here: 30.7 us
  Pallas kernels  17 us (55%)
  starting transfers between devices  8.65 us (28%)
  waiting for transfers between devices  3.62 us (12%)
  between operations  1.44 us (5%)
    pallas_call x5, Pallas kernels, call(): pl.pallas_call(kernel, out_shape=[jax.ShapeDtypeStruct(shape, F32) for sh...  17 us
    ppermute x1, starting transfers between devices, on_device(): got_a = lax.ppermute(rows_a, axes, pairs_a)  5.52 us
    ppermute x1, waiting for transfers between devices, on_device(): lon_b = lax.ppermute(cols_b, axes, pairs_b)  3.61 us
    ppermute x1, starting transfers between devices, on_device(): got_b = lax.ppermute(rows_b, axes, pairs_b)  2.36 us
  transfers between devices with their start and end apart: 4, of which 1 were waited for; matrix products, arithmetic and copies ran while one was open for 0% of the time, Pallas kernels for 32%

profile of v2, /device:TPU:48, one launch (start us, length us, event | category | flops | bytes accessed | tf_op | source)
XLA Modules:
  0.0 30.7 jit_solution(10564181427845570170)
XLA Ops:
  0.6 0.0 copy-start.5
  0.6 0.0 copy-start.4
  0.7 0.0 copy-start.7
  0.7 0.0 copy-start.6
  0.7 0.0 copy-start.3
  0.7 0.0 copy-start.2
  0.7 0.0 copy-start.1
  0.7 0.0 copy-start
  0.7 1.9 %shard_map.129 = (f32[21,8,128]{2,1,0:T(8,128)}, f32[27,8,128]{2,1,0:T(8,128)}) custom-call(f32[8,64,128]{2,1,0:T(8,128)} %refs_0_.1, f32[8,64,128]{2,1,0:T(8,128)} %refs_1_.1, f32[8,64,128]{2,1,0:T(8,128)} %refs_2_.1, f32[8,64,128]{2,1,0:T(8,128)} %refs_3_.2, f32[8,64,128]{2,1,0:T(8,128)} %refs_4_.1, s32[8,64,128]{2,1,0:T(8,128)} %refs_5_.1, ...), custom_call_target="tpu_custom_call" | custom-call | bytes 2000000 | tf_op jit(solution)/shard_map/pallas_call | solution.py:493
  2.6 2.4 %collective-permute-start.1 = (f32[27,8,128]{2,1,0:T(8,128)}, f32[27,8,128]{2,1,0:T(8,128)S(1)}, u32[]{:S(2)}, u32[]{:S(2)}) collective-permute-start(f32[27,8,128]{2,1,0:T(8,128)} %get-tuple-element.16), channel_id=1, source_target_pairs={{16,32},{17,33},{18,34},{19,35},{20,36},{21,37},{22,38},{23,39},{2... | collective-permute-start | bytes 331784 | tf_op jit(solution)/shard_map/ppermute | solution.py:542
  5.0 5.5 %collective-permute-start = (f32[21,8,128]{2,1,0:T(8,128)}, f32[21,8,128]{2,1,0:T(8,128)S(1)}, u32[]{:S(2)}, u32[]{:S(2)}) collective-permute-start(f32[21,8,128]{2,1,0:T(8,128)} %get-tuple-element.15), channel_id=1, source_target_pairs={{0,16},{1,17},{2,18},{3,19},{4,20},{5,21},{6,22},{7,23},{8,24},{9,... | collective-permute-start | bytes 258056 | tf_op jit(solution)/shard_map/ppermute | solution.py:543
  10.5 0.0 copy-done.5
  10.5 0.0 copy-done.4
  10.5 0.0 copy-done.7
  10.5 0.0 copy-done.6
  10.5 0.0 copy-done.3
  10.5 0.0 copy-done.2
  10.5 0.0 copy-done.1
  10.6 0.0 copy-done
  10.6 7.0 %shard_map.128 = (f32[4,66,8,128]{3,2,1,0:T(8,128)S(1)}, f32[2,7,9,8,128]{4,3,2,1,0:T(8,128)S(1)}, f32[2,18,8,128]{3,2,1,0:T(8,128)S(1)}, f32[7,16,8,128]{3,2,1,0:T(8,128)S(1)}) custom-call(f32[512,128]{1,0:T(8,128)S(1)} %bitcast.6, f32[512,128]{1,0:T(8,128)S(1)} %bitcast.7, f32[512,128]{1,0:T(8,128)S(1)} %bitcast.8, f32[512,128]{1,0:T(8,128)S(1)} %bitcast.9, ...), custom_call_target="tpu_custom_call" | custom-call | flops 40000000 | bytes 2000000 | tf_op jit(solution)/shard_map/pallas_call | solution.py:493
  17.5 0.0 collective-permute-done.got_a.refs_1_.refs_3_
  17.6 0.0 collective-permute-done.1.got_b.refs_2_.refs_4_
  17.6 0.2 shard_map.130
  17.8 0.5 %collective-permute-start.2 = (f32[18,8,128]{2,1,0:T(8,128)S(1)}, f32[18,8,128]{2,1,0:T(8,128)S(1)}, u32[]{:S(2)}, u32[]{:S(2)}) collective-permute-start(f32[18,8,128]{2,1,0:T(8,128)S(1)} %get-tuple-element.17), channel_id=1, source_target_pairs={{0,1},{1,0},{2,3},{3,2},{4,5},{5,4},{6,7},{7,6},{8,9},{9,8},{10,11... | collective-permute-start | bytes 221192 | tf_op jit(solution)/shard_map/ppermute | solution.py:555
  18.2 0.3 collective-permute-start.3
  19.2 2.8 %shard_map.131.refs_6_ = f32[4,8,8,128]{3,2,1,0:T(8,128)S(1)} custom-call(f32[7,16,8,128]{3,2,1,0:T(8,128)S(1)} %get-tuple-element.20.refs_0_, f32[21,8,128]{2,1,0:T(8,128)S(1)} %collective-permute-done.got_a.refs_1_.refs_3_, f32[27,8,128]{2,1,0:T(8,128)S(1)} %collective-permute-done.1.got_b.refs_2_.refs_4_, s32[1]{0:T(128)S(6)} %copy.14.refs_3_.refs_7_), custom_call_target="tpu_custom_call" | custom-call | flops 10000000 | bytes 2000000 | tf_op jit(solution)/shard_map/pallas_call | solution.py:493
  22.0 0.0 collective-permute-done.2.refs_1_
  22.0 3.6 %collective-permute-done.3.refs_2_ = f32[18,8,128]{2,1,0:T(8,128)S(1)} collective-permute-done((f32[18,8,128]{2,1,0:T(8,128)S(1)}, f32[18,8,128]{2,1,0:T(8,128)S(1)}, u32[]{:S(2)}, u32[]{:S(2)}) %collective-permute-start.3) | collective-permute-done | bytes 73760 | tf_op jit(solution)/shard_map/ppermute | solution.py:554
  25.6 5.1 %shard_map.132 = (f32[8,64,128]{2,1,0:T(8,128)}, f32[8,64,128]{2,1,0:T(8,128)}, f32[8,64,128]{2,1,0:T(8,128)}, f32[8,64,128]{2,1,0:T(8,128)}, f32[8,64,128]{2,1,0:T(8,128)}) custom-call(f32[2,7,9,8,128]{4,3,2,1,0:T(8,128)S(1)} %get-tuple-element.13.refs_0_, f32[18,8,128]{2,1,0:T(8,128)S(1)} %collective-permute-done.2.refs_1_, ...), custom_call_target="tpu_custom_call" | custom-call | flops 10000000 | bytes 2000000 | tf_op jit(solution)/shard_map/pallas_call | solution.py:493
Async XLA Ops:
  0.6 9.9 %copy-start.5 = (s32[8,64,128]{2,1,0:T(8,128)S(1)}, s32[8,64,128]{2,1,0:T(8,128)}, u32[]{:S(2)}) copy-start(s32[8,64,128]{2,1,0:T(8,128)} %refs_5_.1) | copy-start | bytes 786436
  0.6 9.9 %copy-start.4 = (f32[8,64,128]{2,1,0:T(8,128)S(1)}, f32[8,64,128]{2,1,0:T(8,128)}, u32[]{:S(2)}) copy-start(f32[8,64,128]{2,1,0:T(8,128)} %refs_4_.1) | copy-start | bytes 786436
  0.7 9.9 %copy-start.7 = (f32[64,128]{1,0:T(8,128)S(1)}, f32[64,128]{1,0:T(8,128)}, u32[]{:S(2)}) copy-start(f32[64,128]{1,0:T(8,128)} %refs_7_.4) | copy-start | bytes 98308
  0.7 9.9 %copy-start.6 = (f32[64,128]{1,0:T(8,128)S(1)}, f32[64,128]{1,0:T(8,128)}, u32[]{:S(2)}) copy-start(f32[64,128]{1,0:T(8,128)} %refs_6_.3) | copy-start | bytes 98308
  0.7 9.9 %copy-start.3 = (f32[8,64,128]{2,1,0:T(8,128)S(1)}, f32[8,64,128]{2,1,0:T(8,128)}, u32[]{:S(2)}) copy-start(f32[8,64,128]{2,1,0:T(8,128)} %refs_3_.2) | copy-start | bytes 786436
  0.7 9.9 %copy-start.2 = (f32[8,64,128]{2,1,0:T(8,128)S(1)}, f32[8,64,128]{2,1,0:T(8,128)}, u32[]{:S(2)}) copy-start(f32[8,64,128]{2,1,0:T(8,128)} %refs_2_.1) | copy-start | bytes 786436
  0.7 9.9 %copy-start.1 = (f32[8,64,128]{2,1,0:T(8,128)S(1)}, f32[8,64,128]{2,1,0:T(8,128)}, u32[]{:S(2)}) copy-start(f32[8,64,128]{2,1,0:T(8,128)} %refs_1_.1) | copy-start | bytes 786436
  0.7 9.9 %copy-start = (f32[8,64,128]{2,1,0:T(8,128)S(1)}, f32[8,64,128]{2,1,0:T(8,128)}, u32[]{:S(2)}) copy-start(f32[8,64,128]{2,1,0:T(8,128)} %refs_0_.1) | copy-start | bytes 786436
  2.6 14.9 %collective-permute-start.1 = (f32[27,8,128]{2,1,0:T(8,128)}, f32[27,8,128]{2,1,0:T(8,128)S(1)}, u32[]{:S(2)}, u32[]{:S(2)}) collective-permute-start(f32[27,8,128]{2,1,0:T(8,128)} %get-tuple-element.16), channel_id=1, source_target_pairs={{16,32},{17,33},{18,34},{19,35},{20,36},{21,37},{22,38},{23,39},{2... | collective-permute-start | bytes 331784 | tf_op jit(solution)/shard_map/ppermute | solution.py:542
  5.0 12.6 %collective-permute-start = (f32[21,8,128]{2,1,0:T(8,128)}, f32[21,8,128]{2,1,0:T(8,128)S(1)}, u32[]{:S(2)}, u32[]{:S(2)}) collective-permute-start(f32[21,8,128]{2,1,0:T(8,128)} %get-tuple-element.15), channel_id=1, source_target_pairs={{0,16},{1,17},{2,18},{3,19},{4,20},{5,21},{6,22},{7,23},{8,24},{9,... | collective-permute-start | bytes 258056 | tf_op jit(solution)/shard_map/ppermute | solution.py:543
  17.8 4.3 %collective-permute-start.2 = (f32[18,8,128]{2,1,0:T(8,128)S(1)}, f32[18,8,128]{2,1,0:T(8,128)S(1)}, u32[]{:S(2)}, u32[]{:S(2)}) collective-permute-start(f32[18,8,128]{2,1,0:T(8,128)S(1)} %get-tuple-element.17), channel_id=1, source_target_pairs={{0,1},{1,0},{2,3},{3,2},{4,5},{5,4},{6,7},{7,6},{8,9},{9,8},{10,11... | collective-permute-start | bytes 221192 | tf_op jit(solution)/shard_map/ppermute | solution.py:555
  18.2 7.4 %collective-permute-start.3 = (f32[18,8,128]{2,1,0:T(8,128)S(1)}, f32[18,8,128]{2,1,0:T(8,128)S(1)}, u32[]{:S(2)}, u32[]{:S(2)}) collective-permute-start(f32[18,8,128]{2,1,0:T(8,128)S(1)} %get-tuple-element.18), channel_id=1, source_target_pairs={{0,15},{1,2},{2,1},{3,4},{4,3},{5,6},{6,5},{7,8},{8,7},{9,10},{10,... | collective-permute-start | bytes 221192 | tf_op jit(solution)/shard_map/ppermute | solution.py:554

commit v3 on v2

--- a/solution.py
+++ b/solution.py
@@ -25,7 +25,6 @@
 eos_cross = 0.0024341
 
 SIGNS = (1.0, 1.0, -1.0, -1.0)
-MIB = 1024 * 1024
 
 
 def roll(x, shift):
@@ -42,12 +41,7 @@
 
 
 def mirrored(x, width):
-    lane = lanes()
-    bit = 1
-    while bit < width:
-        x = jnp.where((lane & bit) != 0, roll(x, bit), roll(x, -bit))
-        bit *= 2
-    return x
+    return jnp.take_along_axis(x, lanes() ^ (width - 1), axis=1, mode="promise_in_bounds")
 
 
 def eos_terms():
@@ -374,7 +368,7 @@
 
 
 def columns_strip_kernel(*refs):
-    own, lon_a, lon_b, got_a, got_b, inner, strips, hinge = refs[:8]
+    own, lon_b, lon_a, got_a, got_b, inner, strips, hinge = refs[:8]
     outs = refs[8:13]
     state = refs[13:17]
     east_w, north_w = refs[17:19]
@@ -476,27 +470,35 @@
         new.append(density_of(new[0], new[1], terms))
         for ref, value in zip(stage, new):
             ref.reshape(LEVELS * ROWS, LANES)[pl.ds(row, LEVELS, stride=ROWS), :] = value
-        if row % 8 == 7:
-            rows = pl.ds(row - 7, 8)
+        if row % 16 == 15:
+            rows = pl.ds(row - 15, 16)
             for f in range(5):
-                copy = pltpu.make_async_copy(stage[f].at[:, rows, :], outs[f].at[:, rows, :], sems.at[f, row // 8])
+                copy = pltpu.make_async_copy(stage[f].at[:, rows, :], outs[f].at[:, rows, :], sems.at[f, row // 16])
                 copy.start()
                 copies.append(copy)
     for copy in copies:
         copy.wait()
 
 
-def call(kernel, ins, outs, scratch=(), smem_last=False, far=False, out_far=False, flops=0, limit=40):
-    specs = [pl.BlockSpec(memory_space=pltpu.HBM if far else pltpu.VMEM) for _ in ins]
+def call(kernel, ins, outs, scratch=(), smem_last=False, far=False, out_far=False, flops=0):
+    place = pltpu.HBM if far else pltpu.VMEM
+    specs = [pl.BlockSpec(memory_space=place) for _ in ins]
+    ins = [pltpu.with_memory_space_constraint(x, place) for x in ins[:-1]] + [ins[-1]]
     if smem_last:
         specs[-1] = pl.BlockSpec(memory_space=pltpu.SMEM)
+    else:
+        ins[-1] = pltpu.with_memory_space_constraint(ins[-1], place)
+    if out_far:
+        out_shape = [jax.ShapeDtypeStruct(shape, F32) for shape in outs]
+    else:
+        out_shape = [pltpu.VMEM(shape, F32) for shape in outs]
     return pl.pallas_call(
         kernel,
-        out_shape=[jax.ShapeDtypeStruct(shape, F32) for shape in outs],
+        out_shape=out_shape,
         in_specs=specs,
         out_specs=[pl.BlockSpec(memory_space=pltpu.HBM if out_far else pltpu.VMEM) for _ in outs],
         scratch_shapes=list(scratch),
-        compiler_params=pltpu.CompilerParams(vmem_limit_bytes=limit * MIB),
+        compiler_params=pltpu.CompilerParams(vmem_limit_bytes=40 * 1024 * 1024),
         cost_estimate=pl.CostEstimate(flops=flops, bytes_accessed=2_000_000, transcendentals=0),
     )(*ins)
 
@@ -536,7 +538,6 @@
         + [pltpu.VMEM((2,) + tile, F32)] * 2
         + [pltpu.SemaphoreType.DMA((8, 2))],
         far=True,
-        limit=54,
     )
     pairs_a, pairs_b = lat_pairs(lat, lon)
     got_b = lax.ppermute(rows_b, axes, pairs_b)
@@ -547,7 +548,6 @@
         [(4, ROWS + 2) + tile, (2, 7, BLOCK) + tile, (2, 2 * BLOCK) + tile, (7, 16) + tile],
         geo_scratch(ROWS + 2),
         flops=40_000_000,
-        limit=50,
     )
     cols_a, cols_b = call(columns_kernel, [msgs, got_a, got_b], [(2 * BLOCK,) + tile] * 2)
     pairs_a, pairs_b = lon_pairs(lat, lon)
@@ -563,12 +563,12 @@
     )
     outs = call(
         columns_strip_kernel,
-        [own, lon_a, lon_b, got_a, got_b, inner, strips, hinge],
+        [own, lon_b, lon_a, got_a, got_b, inner, strips, hinge],
         [(LEVELS, ROWS, LANES)] * 5,
         state_scratch(WE_ROWS)
         + geo_scratch(WE_ROWS)
         + [pltpu.VMEM((LEVELS, ROWS, LANES), F32)] * 5
-        + [pltpu.SemaphoreType.DMA((5, 8))],
+        + [pltpu.SemaphoreType.DMA((5, 4))],
         out_far=True,
         smem_last=True,
         flops=10_000_000,

time: 30.8 us -> 29.2 us (0.948)
  Pallas kernels: 17 us -> 14.1 us
  waiting for transfers between devices: 3.62 us -> 4.81 us
    pallas_call x5, Pallas kernels: 17 us -> 14.1 us  [call(): pl.pallas_call(kernel, out_shape=out_shape, in_specs=specs, out_specs=[pl...]
    ppermute x1, waiting for transfers between devices: 3.61 us -> 4.8 us  [on_device(): lon_b = lax.ppermute(cols_b, axes, pairs_b)]
  transfers between devices with their start and end apart: 4 -> 4, of which waited for: 1 -> 1; matrix products, arithmetic and copies ran while one was open for 0% -> 0% of each run, Pallas kernels for 32% -> 29%
where the time goes in v3:
time: 29.2 us; the launch traced here: 29 us
  Pallas kernels  14.1 us (48%)
  starting transfers between devices  8.63 us (30%)
  waiting for transfers between devices  4.81 us (16%)
  between operations  1.44 us (5%)
    pallas_call x5, Pallas kernels, call(): pl.pallas_call(kernel, out_shape=out_shape, in_specs=specs, out_specs=[pl...  14.1 us
    ppermute x1, starting transfers between devices, on_device(): got_a = lax.ppermute(rows_a, axes, pairs_a)  5.52 us
    ppermute x1, waiting for transfers between devices, on_device(): lon_b = lax.ppermute(cols_b, axes, pairs_b)  4.8 us
    ppermute x1, starting transfers between devices, on_device(): got_b = lax.ppermute(rows_b, axes, pairs_b)  2.36 us
  transfers between devices with their start and end apart: 4, of which 1 were waited for; matrix products, arithmetic and copies ran while one was open for 0% of the time, Pallas kernels for 29%

profile of v3, /device:TPU:48, one launch (start us, length us, event | category | flops | bytes accessed | tf_op | source)
XLA Modules:
  0.0 29.0 jit_solution(14823303823684982604)
XLA Ops:
  0.6 0.0 copy-start.5
  0.6 0.0 copy-start.4
  0.7 0.0 copy-start.7
  0.7 0.0 copy-start.6
  0.7 0.0 copy-start.3
  0.7 0.0 copy-start.2
  0.7 0.0 copy-start.1
  0.7 0.0 copy-start
  0.7 1.2 %shard_map.129 = (f32[21,8,128]{2,1,0:T(8,128)S(1)}, f32[27,8,128]{2,1,0:T(8,128)S(1)}) custom-call(f32[8,64,128]{2,1,0:T(8,128)} %refs_0_.1, f32[8,64,128]{2,1,0:T(8,128)} %refs_1_.1, f32[8,64,128]{2,1,0:T(8,128)} %refs_2_.1, f32[8,64,128]{2,1,0:T(8,128)} %refs_3_.2, f32[8,64,128]{2,1,0:T(8,128)} %refs_4_.1, s32[8,64,128]{2,1,0:T(8,128)} %refs_5_.1, ...), custom_call_target="tpu_custom_call" | custom-call | bytes 2000000 | tf_op jit(solution)/shard_map/pallas_call | solution.py:495
  2.0 2.4 %collective-permute-start.1 = (f32[27,8,128]{2,1,0:T(8,128)S(1)}, f32[27,8,128]{2,1,0:T(8,128)S(1)}, u32[]{:S(2)}, u32[]{:S(2)}) collective-permute-start(f32[27,8,128]{2,1,0:T(8,128)S(1)} %get-tuple-element.16), channel_id=1, source_target_pairs={{16,32},{17,33},{18,34},{19,35},{20,36},{21,37},{22,38},{23,39},{2... | collective-permute-start | bytes 331784 | tf_op jit(solution)/shard_map/ppermute | solution.py:543
  4.3 5.5 %collective-permute-start = (f32[21,8,128]{2,1,0:T(8,128)S(1)}, f32[21,8,128]{2,1,0:T(8,128)S(1)}, u32[]{:S(2)}, u32[]{:S(2)}) collective-permute-start(f32[21,8,128]{2,1,0:T(8,128)S(1)} %get-tuple-element.15), channel_id=1, source_target_pairs={{0,16},{1,17},{2,18},{3,19},{4,20},{5,21},{6,22},{7,23},{8,24},{9,... | collective-permute-start | bytes 258056 | tf_op jit(solution)/shard_map/ppermute | solution.py:544
  9.8 0.0 copy-done.5
  9.8 0.0 copy-done.4
  9.8 0.0 copy-done.7
  9.9 0.0 copy-done.6
  9.9 0.0 copy-done.3
  9.9 0.0 copy-done.2
  9.9 0.0 copy-done.1
  9.9 0.0 copy-done
  9.9 7.1 %shard_map.128 = (f32[4,66,8,128]{3,2,1,0:T(8,128)S(1)}, f32[2,7,9,8,128]{4,3,2,1,0:T(8,128)S(1)}, f32[2,18,8,128]{3,2,1,0:T(8,128)S(1)}, f32[7,16,8,128]{3,2,1,0:T(8,128)S(1)}) custom-call(f32[512,128]{1,0:T(8,128)S(1)} %bitcast.6, f32[512,128]{1,0:T(8,128)S(1)} %bitcast.7, f32[512,128]{1,0:T(8,128)S(1)} %bitcast.8, f32[512,128]{1,0:T(8,128)S(1)} %bitcast.9, ...), custom_call_target="tpu_custom_call" | custom-call | flops 40000000 | bytes 2000000 | tf_op jit(solution)/shard_map/pallas_call | solution.py:495
  17.0 0.0 collective-permute-done.got_a.refs_1_.refs_3_
  17.0 0.0 collective-permute-done.1.got_b.refs_2_.refs_4_
  17.0 0.2 shard_map.130
  17.2 0.5 %collective-permute-start.2 = (f32[18,8,128]{2,1,0:T(8,128)S(1)}, f32[18,8,128]{2,1,0:T(8,128)S(1)}, u32[]{:S(2)}, u32[]{:S(2)}) collective-permute-start(f32[18,8,128]{2,1,0:T(8,128)S(1)} %get-tuple-element.17), channel_id=1, source_target_pairs={{0,15},{1,2},{2,1},{3,4},{4,3},{5,6},{6,5},{7,8},{8,7},{9,10},{10,... | collective-permute-start | bytes 221192 | tf_op jit(solution)/shard_map/ppermute | solution.py:554
  17.7 0.2 collective-permute-start.3
  18.6 1.3 %shard_map.131.refs_6_ = f32[4,8,8,128]{3,2,1,0:T(8,128)S(1)} custom-call(f32[7,16,8,128]{3,2,1,0:T(8,128)S(1)} %get-tuple-element.20.refs_0_, f32[21,8,128]{2,1,0:T(8,128)S(1)} %collective-permute-done.got_a.refs_1_.refs_3_, f32[27,8,128]{2,1,0:T(8,128)S(1)} %collective-permute-done.1.got_b.refs_2_.refs_4_, s32[1]{0:T(128)S(6)} %copy.14.refs_3_.refs_7_), custom_call_target="tpu_custom_call" | custom-call | flops 10000000 | bytes 2000000 | tf_op jit(solution)/shard_map/pallas_call | solution.py:495
  19.9 4.8 %collective-permute-done.2.refs_1_ = f32[18,8,128]{2,1,0:T(8,128)S(1)} collective-permute-done((f32[18,8,128]{2,1,0:T(8,128)S(1)}, f32[18,8,128]{2,1,0:T(8,128)S(1)}, u32[]{:S(2)}, u32[]{:S(2)}) %collective-permute-start.2) | collective-permute-done | bytes 73760 | tf_op jit(solution)/shard_map/ppermute | solution.py:554
  24.7 0.0 collective-permute-done.3.refs_2_
  24.7 4.3 %shard_map.132 = (f32[8,64,128]{2,1,0:T(8,128)}, f32[8,64,128]{2,1,0:T(8,128)}, f32[8,64,128]{2,1,0:T(8,128)}, f32[8,64,128]{2,1,0:T(8,128)}, f32[8,64,128]{2,1,0:T(8,128)}) custom-call(f32[2,7,9,8,128]{4,3,2,1,0:T(8,128)S(1)} %get-tuple-element.13.refs_0_, f32[18,8,128]{2,1,0:T(8,128)S(1)} %collective-permute-done.2.refs_1_, ...), custom_call_target="tpu_custom_call" | custom-call | flops 10000000 | bytes 2000000 | tf_op jit(solution)/shard_map/pallas_call | solution.py:495
Async XLA Ops:
  0.6 9.2 %copy-start.5 = (s32[8,64,128]{2,1,0:T(8,128)S(1)}, s32[8,64,128]{2,1,0:T(8,128)}, u32[]{:S(2)}) copy-start(s32[8,64,128]{2,1,0:T(8,128)} %refs_5_.1) | copy-start | bytes 786436
  0.6 9.2 %copy-start.4 = (f32[8,64,128]{2,1,0:T(8,128)S(1)}, f32[8,64,128]{2,1,0:T(8,128)}, u32[]{:S(2)}) copy-start(f32[8,64,128]{2,1,0:T(8,128)} %refs_4_.1) | copy-start | bytes 786436
  0.7 9.2 %copy-start.7 = (f32[64,128]{1,0:T(8,128)S(1)}, f32[64,128]{1,0:T(8,128)}, u32[]{:S(2)}) copy-start(f32[64,128]{1,0:T(8,128)} %refs_7_.4) | copy-start | bytes 98308
  0.7 9.2 %copy-start.6 = (f32[64,128]{1,0:T(8,128)S(1)}, f32[64,128]{1,0:T(8,128)}, u32[]{:S(2)}) copy-start(f32[64,128]{1,0:T(8,128)} %refs_6_.3) | copy-start | bytes 98308
  0.7 9.2 %copy-start.3 = (f32[8,64,128]{2,1,0:T(8,128)S(1)}, f32[8,64,128]{2,1,0:T(8,128)}, u32[]{:S(2)}) copy-start(f32[8,64,128]{2,1,0:T(8,128)} %refs_3_.2) | copy-start | bytes 786436
  0.7 9.2 %copy-start.2 = (f32[8,64,128]{2,1,0:T(8,128)S(1)}, f32[8,64,128]{2,1,0:T(8,128)}, u32[]{:S(2)}) copy-start(f32[8,64,128]{2,1,0:T(8,128)} %refs_2_.1) | copy-start | bytes 786436
  0.7 9.2 %copy-start.1 = (f32[8,64,128]{2,1,0:T(8,128)S(1)}, f32[8,64,128]{2,1,0:T(8,128)}, u32[]{:S(2)}) copy-start(f32[8,64,128]{2,1,0:T(8,128)} %refs_1_.1) | copy-start | bytes 786436
  0.7 9.2 %copy-start = (f32[8,64,128]{2,1,0:T(8,128)S(1)}, f32[8,64,128]{2,1,0:T(8,128)}, u32[]{:S(2)}) copy-start(f32[8,64,128]{2,1,0:T(8,128)} %refs_0_.1) | copy-start | bytes 786436
  2.0 15.0 %collective-permute-start.1 = (f32[27,8,128]{2,1,0:T(8,128)S(1)}, f32[27,8,128]{2,1,0:T(8,128)S(1)}, u32[]{:S(2)}, u32[]{:S(2)}) collective-permute-start(f32[27,8,128]{2,1,0:T(8,128)S(1)} %get-tuple-element.16), channel_id=1, source_target_pairs={{16,32},{17,33},{18,34},{19,35},{20,36},{21,37},{22,38},{23,39},{2... | collective-permute-start | bytes 331784 | tf_op jit(solution)/shard_map/ppermute | solution.py:543
  4.3 12.7 %collective-permute-start = (f32[21,8,128]{2,1,0:T(8,128)S(1)}, f32[21,8,128]{2,1,0:T(8,128)S(1)}, u32[]{:S(2)}, u32[]{:S(2)}) collective-permute-start(f32[21,8,128]{2,1,0:T(8,128)S(1)} %get-tuple-element.15), channel_id=1, source_target_pairs={{0,16},{1,17},{2,18},{3,19},{4,20},{5,21},{6,22},{7,23},{8,24},{9,... | collective-permute-start | bytes 258056 | tf_op jit(solution)/shard_map/ppermute | solution.py:544
  17.2 7.5 %collective-permute-start.2 = (f32[18,8,128]{2,1,0:T(8,128)S(1)}, f32[18,8,128]{2,1,0:T(8,128)S(1)}, u32[]{:S(2)}, u32[]{:S(2)}) collective-permute-start(f32[18,8,128]{2,1,0:T(8,128)S(1)} %get-tuple-element.17), channel_id=1, source_target_pairs={{0,15},{1,2},{2,1},{3,4},{4,3},{5,6},{6,5},{7,8},{8,7},{9,10},{10,... | collective-permute-start | bytes 221192 | tf_op jit(solution)/shard_map/ppermute | solution.py:554
  17.7 6.9 %collective-permute-start.3 = (f32[18,8,128]{2,1,0:T(8,128)S(1)}, f32[18,8,128]{2,1,0:T(8,128)S(1)}, u32[]{:S(2)}, u32[]{:S(2)}) collective-permute-start(f32[18,8,128]{2,1,0:T(8,128)S(1)} %get-tuple-element.18), channel_id=1, source_target_pairs={{0,1},{1,0},{2,3},{3,2},{4,5},{5,4},{6,7},{7,6},{8,9},{9,8},{10,11... | collective-permute-start | bytes 221192 | tf_op jit(solution)/shard_map/ppermute | solution.py:555

commit v4 on v3

--- a/solution.py
+++ b/solution.py
@@ -88,7 +88,7 @@
     geo["inv"][row] = (0.5 * time_step) / (east0 * north0 * jnp.where(half0 > 0.0, half0, 1.0))
 
 
-def march(state, geo, chains):
+def march(state, geo, chains, target=None):
     terms = eos_terms()
 
     def north_face(row, speed):
@@ -120,7 +120,7 @@
         ]
         new[2] = (new[2] + (press - roll(press, -1)) * geo["push_e"][row]) * geo["open_e"][row]
         new[3] = (new[3] + (press - press_n) * geo["push_n"][row]) * geo["open_n"][row]
-        for ref, value in zip(state, new):
+        for ref, value in zip(state if target is None else target, new):
             ref[row] = value
         return here + north + (north_p, north_m, press_n)
 
@@ -217,9 +217,10 @@
 
 def interior_kernel(*refs):
     ins = refs[:8]
-    state_out, own, msgs, rims = refs[8:12]
+    state_out, own, msgs, rims, geo_out = refs[8:13]
     state = [state_out.at[f] for f in range(4)]
-    geo = dict(zip(GEO, refs[12:22]))
+    geo = {name: geo_out.at[index] for index, name in enumerate(GEO)}
+    spread = refs[13:15]
     blank = jnp.zeros((LEVELS, LANES), F32)
     for ref in state + [geo["half"]]:
         ref[0] = blank
@@ -230,6 +231,8 @@
         for ref, value in zip(state, values):
             ref[row + 1] = value
         geo["half"][row + 1] = values[4]
+        spread[0][row + 1] = wide(ins[6], row)
+        spread[1][row + 1] = wide(ins[7], row)
         return carry
 
     lax.fori_loop(0, ROWS, take, 0, unroll=8)
@@ -238,11 +241,11 @@
             for f in range(4):
                 rims[f, place] = state[f][row + 1]
             rims[4, place] = geo["half"][row + 1]
-            rims[5, place] = wide(ins[6], row)
-            rims[6, place] = wide(ins[7], row)
+            rims[5, place] = spread[0][row + 1]
+            rims[6, place] = spread[1][row + 1]
 
     lane = lanes()
-    part = (lane // HALO) % (GROUP // HALO)
+    part = (lane >> 2) & 3
 
     def pack(g, carry):
         packs = []
@@ -255,8 +258,8 @@
                 elif f == 4:
                     value = geo["half"][row + 1]
                 else:
-                    value = wide(ins[f + 1], row)
-                here = (lane // GROUP) == q
+                    value = spread[f - 5][row + 1]
+                here = (lane >> 4) == q
                 west = jnp.where(here, roll(value, GROUP * q + HALO), west)
                 east = jnp.where(here, roll(value, GROUP * q + 12), east)
             own[0, f, g] = west
@@ -275,7 +278,7 @@
     lax.fori_loop(0, BLOCK, pack, 0, unroll=3)
 
     def shape(row, carry):
-        geometry_row(geo, row + 1, wide(ins[6], row), wide(ins[7], row), wide(ins[6], row + 1), wide(ins[7], row + 1))
+        geometry_row(geo, row + 1, spread[0][row + 1], spread[1][row + 1], spread[0][row + 2], spread[1][row + 2])
         return carry
 
     lax.fori_loop(0, ROWS - 1, shape, 0, unroll=7)
@@ -284,7 +287,7 @@
         march(state, geo, ((2, ROWS - 2),))
         return carry
 
-    lax.fori_loop(1, NSTEP + 1, step, 0)
+    lax.fori_loop(1, NSTEP, step, 0)
 
 
 def columns_kernel(msgs, got_a, got_b, out_a, out_b):
@@ -292,7 +295,7 @@
     top = lax.axis_index("lat") == lax.axis_size("lat") - 1
     south, north, fold = halo_rows(got_a, got_b)
     lane = lanes()
-    part = (lane // HALO) % (GROUP // HALO)
+    part = (lane >> 2) & 3
     for half, first in ((0, 0), (1, 4)):
         for g in range(BLOCK):
             slot = BLOCK * half + g
@@ -322,10 +325,10 @@
 
 
 def rows_strip_kernel(*refs):
-    rims, got_a, got_b, hinge, out = refs[:5]
-    state = refs[5:9]
-    east_w, north_w = refs[9:11]
-    geo = dict(zip(GEO, refs[11:]))
+    inner, inner_geo, rims, got_a, got_b, hinge, out, inner_out = refs[:8]
+    state = refs[8:12]
+    east_w, north_w = refs[12:14]
+    geo = dict(zip(GEO, refs[14:]))
     top = lax.axis_index("lat") == lax.axis_size("lat") - 1
     pivot = hinge[0]
     south, north, fold = halo_rows(got_a, got_b)
@@ -358,6 +361,13 @@
             chains.append((FOLD + s, 5 - s))
         march(state, geo, chains)
 
+    march(
+        [inner.at[f] for f in range(4)],
+        {name: inner_geo.at[index] for index, name in enumerate(GEO)},
+        ((HALO + 1, ROWS - 2 * HALO),),
+        [inner_out.at[f] for f in range(4)],
+    )
+
     for f, ref in enumerate(state):
         for i in range(HALO):
             out[f, i] = ref[SOUTH + HALO + i]
@@ -380,7 +390,7 @@
     south, north, fold = halo_rows(got_a, got_b)
     fields = list(state) + [geo["half"], east_w, north_w]
     lane = lanes()
-    inside = lane % GROUP
+    inside = lane & (GROUP - 1)
 
     def message(side, f, g):
         slot = g if f < 4 else BLOCK + g
@@ -542,21 +552,21 @@
     pairs_a, pairs_b = lat_pairs(lat, lon)
     got_b = lax.ppermute(rows_b, axes, pairs_b)
     got_a = lax.ppermute(rows_a, axes, pairs_a)
-    inner, own, msgs, rims = call(
+    inner, own, msgs, rims, inner_geo = call(
         interior_kernel,
         flat,
-        [(4, ROWS + 2) + tile, (2, 7, BLOCK) + tile, (2, 2 * BLOCK) + tile, (7, 16) + tile],
-        geo_scratch(ROWS + 2),
+        [(4, ROWS + 2) + tile, (2, 7, BLOCK) + tile, (2, 2 * BLOCK) + tile, (7, 16) + tile, (len(GEO), ROWS + 2) + tile],
+        [pltpu.VMEM((ROWS + 2,) + tile, F32)] * 2,
         flops=40_000_000,
     )
     cols_a, cols_b = call(columns_kernel, [msgs, got_a, got_b], [(2 * BLOCK,) + tile] * 2)
     pairs_a, pairs_b = lon_pairs(lat, lon)
     lon_b = lax.ppermute(cols_b, axes, pairs_b)
     lon_a = lax.ppermute(cols_a, axes, pairs_a)
-    (strips,) = call(
+    strips, inner = call(
         rows_strip_kernel,
-        [rims, got_a, got_b, hinge],
-        [(4, 2 * HALO) + tile],
+        [inner, inner_geo, rims, got_a, got_b, hinge],
+        [(4, 2 * HALO) + tile, (4, ROWS + 2) + tile],
         state_scratch(NS_ROWS) + geo_scratch(NS_ROWS),
         smem_last=True,
         flops=10_000_000,

time: 29.2 us -> 28.3 us (0.969)
  waiting for transfers between devices: 4.81 us -> 4.16 us
  Pallas kernels: 14.1 us -> 13.8 us
    ppermute x1, waiting for transfers between devices: 4.8 us -> 4.15 us  [on_device(): lon_b = lax.ppermute(cols_b, axes, pairs_b)]
where the time goes in v4:
time: 28.3 us; the launch traced here: 28.1 us
  Pallas kernels  13.8 us (49%)
  starting transfers between devices  8.63 us (30%)
  waiting for transfers between devices  4.16 us (15%)
  between operations  1.44 us (5%)
    pallas_call x5, Pallas kernels, call(): pl.pallas_call(kernel, out_shape=out_shape, in_specs=specs, out_specs=[pl...  13.8 us
    ppermute x1, starting transfers between devices, on_device(): got_a = lax.ppermute(rows_a, axes, pairs_a)  5.52 us
    ppermute x1, waiting for transfers between devices, on_device(): lon_b = lax.ppermute(cols_b, axes, pairs_b)  4.15 us
    ppermute x1, starting transfers between devices, on_device(): got_b = lax.ppermute(rows_b, axes, pairs_b)  2.36 us
  transfers between devices with their start and end apart: 4, of which 1 were waited for; matrix products, arithmetic and copies ran while one was open for 0% of the time, Pallas kernels for 29%

profile of v4, /device:TPU:48, one launch (start us, length us, event | category | flops | bytes accessed | tf_op | source)
XLA Modules:
  0.0 28.1 jit_solution(8369528620211600692)
XLA Ops:
  0.6 0.0 copy-start.5
  0.6 0.0 copy-start.4
  0.7 0.0 copy-start.7
  0.7 0.0 copy-start.6
  0.7 0.0 copy-start.3
  0.7 0.0 copy-start.2
  0.7 0.0 copy-start.1
  0.7 0.0 copy-start
  0.7 1.2 %shard_map.129 = (f32[21,8,128]{2,1,0:T(8,128)S(1)}, f32[27,8,128]{2,1,0:T(8,128)S(1)}) custom-call(f32[8,64,128]{2,1,0:T(8,128)} %refs_0_.1, f32[8,64,128]{2,1,0:T(8,128)} %refs_1_.1, f32[8,64,128]{2,1,0:T(8,128)} %refs_2_.1, f32[8,64,128]{2,1,0:T(8,128)} %refs_3_.1, f32[8,64,128]{2,1,0:T(8,128)} %refs_4_.1, s32[8,64,128]{2,1,0:T(8,128)} %refs_5_.2, ...), custom_call_target="tpu_custom_call" | custom-call | bytes 2000000 | tf_op jit(solution)/shard_map/pallas_call | solution.py:505
  2.0 2.4 %collective-permute-start.1 = (f32[27,8,128]{2,1,0:T(8,128)S(1)}, f32[27,8,128]{2,1,0:T(8,128)S(1)}, u32[]{:S(2)}, u32[]{:S(2)}) collective-permute-start(f32[27,8,128]{2,1,0:T(8,128)S(1)} %get-tuple-element.19), channel_id=1, source_target_pairs={{16,32},{17,33},{18,34},{19,35},{20,36},{21,37},{22,38},{23,39},{2... | collective-permute-start | bytes 331784 | tf_op jit(solution)/shard_map/ppermute | solution.py:553
  4.3 5.5 %collective-permute-start = (f32[21,8,128]{2,1,0:T(8,128)S(1)}, f32[21,8,128]{2,1,0:T(8,128)S(1)}, u32[]{:S(2)}, u32[]{:S(2)}) collective-permute-start(f32[21,8,128]{2,1,0:T(8,128)S(1)} %get-tuple-element.18), channel_id=1, source_target_pairs={{0,16},{1,17},{2,18},{3,19},{4,20},{5,21},{6,22},{7,23},{8,24},{9,... | collective-permute-start | bytes 258056 | tf_op jit(solution)/shard_map/ppermute | solution.py:554
  9.8 0.0 copy-done.5
  9.8 0.0 copy-done.4
  9.8 0.0 copy-done.7
  9.9 0.0 copy-done.6
  9.9 0.0 copy-done.3
  9.9 0.0 copy-done.2
  9.9 0.0 copy-done.1
  9.9 0.0 copy-done
  9.9 6.2 %shard_map.128 = (f32[4,66,8,128]{3,2,1,0:T(8,128)S(1)}, f32[2,7,9,8,128]{4,3,2,1,0:T(8,128)S(1)}, f32[2,18,8,128]{3,2,1,0:T(8,128)S(1)}, f32[7,16,8,128]{3,2,1,0:T(8,128)S(1)}, f32[10,66,8,128]{3,2,1,0:T(8,128)S(1)}) custom-call(f32[512,128]{1,0:T(8,128)S(1)} %bitcast.6, f32[512,128]{1,0:T(8,128)S(1)} %bitcast.7, f32[512,128]{1,0:T(8,128)S(1)} %bitcast.8, ...), custom_call_target="tpu_custom_call" | custom-call | flops 40000000 | bytes 2000000 | tf_op jit(solution)/shard_map/pallas_call | solution.py:505
  16.1 0.0 collective-permute-done.got_a.refs_3_
  16.1 0.0 collective-permute-done.1.got_b.refs_4_
  16.1 0.2 shard_map.130
  16.3 0.5 %collective-permute-start.2 = (f32[18,8,128]{2,1,0:T(8,128)S(1)}, f32[18,8,128]{2,1,0:T(8,128)S(1)}, u32[]{:S(2)}, u32[]{:S(2)}) collective-permute-start(f32[18,8,128]{2,1,0:T(8,128)S(1)} %get-tuple-element.20), channel_id=1, source_target_pairs={{0,15},{1,2},{2,1},{3,4},{4,3},{5,6},{6,5},{7,8},{8,7},{9,10},{10,... | collective-permute-start | bytes 221192 | tf_op jit(solution)/shard_map/ppermute | solution.py:564
  16.9 0.2 collective-permute-start.3
  17.7 1.9 %shard_map.131 = (f32[4,8,8,128]{3,2,1,0:T(8,128)S(1)}, f32[4,66,8,128]{3,2,1,0:T(8,128)S(1)}) custom-call(f32[4,66,8,128]{3,2,1,0:T(8,128)S(1)} %get-tuple-element.22.refs_0_, f32[10,66,8,128]{3,2,1,0:T(8,128)S(1)} %get-tuple-element.23.refs_1_, f32[7,16,8,128]{3,2,1,0:T(8,128)S(1)} %get-tuple-element.24.refs_2_, ...), custom_call_target="tpu_custom_call" | custom-call | flops 10000000 | bytes 2000000 | tf_op jit(solution)/shard_map/pallas_call | solution.py:505
  19.6 4.2 %collective-permute-done.2.refs_1_ = f32[18,8,128]{2,1,0:T(8,128)S(1)} collective-permute-done((f32[18,8,128]{2,1,0:T(8,128)S(1)}, f32[18,8,128]{2,1,0:T(8,128)S(1)}, u32[]{:S(2)}, u32[]{:S(2)}) %collective-permute-start.2) | collective-permute-done | bytes 73760 | tf_op jit(solution)/shard_map/ppermute | solution.py:564
  23.8 0.0 collective-permute-done.3.refs_2_
  23.8 4.3 %shard_map.132 = (f32[8,64,128]{2,1,0:T(8,128)}, f32[8,64,128]{2,1,0:T(8,128)}, f32[8,64,128]{2,1,0:T(8,128)}, f32[8,64,128]{2,1,0:T(8,128)}, f32[8,64,128]{2,1,0:T(8,128)}) custom-call(f32[2,7,9,8,128]{4,3,2,1,0:T(8,128)S(1)} %get-tuple-element.16.refs_0_, f32[18,8,128]{2,1,0:T(8,128)S(1)} %collective-permute-done.2.refs_1_, ...), custom_call_target="tpu_custom_call" | custom-call | flops 10000000 | bytes 2000000 | tf_op jit(solution)/shard_map/pallas_call | solution.py:505
Async XLA Ops:
  0.6 9.2 %copy-start.5 = (s32[8,64,128]{2,1,0:T(8,128)S(1)}, s32[8,64,128]{2,1,0:T(8,128)}, u32[]{:S(2)}) copy-start(s32[8,64,128]{2,1,0:T(8,128)} %refs_5_.2) | copy-start | bytes 786436
  0.6 9.2 %copy-start.4 = (f32[8,64,128]{2,1,0:T(8,128)S(1)}, f32[8,64,128]{2,1,0:T(8,128)}, u32[]{:S(2)}) copy-start(f32[8,64,128]{2,1,0:T(8,128)} %refs_4_.1) | copy-start | bytes 786436
  0.7 9.2 %copy-start.7 = (f32[64,128]{1,0:T(8,128)S(1)}, f32[64,128]{1,0:T(8,128)}, u32[]{:S(2)}) copy-start(f32[64,128]{1,0:T(8,128)} %refs_7_.4) | copy-start | bytes 98308
  0.7 9.2 %copy-start.6 = (f32[64,128]{1,0:T(8,128)S(1)}, f32[64,128]{1,0:T(8,128)}, u32[]{:S(2)}) copy-start(f32[64,128]{1,0:T(8,128)} %refs_6_.3) | copy-start | bytes 98308
  0.7 9.2 %copy-start.3 = (f32[8,64,128]{2,1,0:T(8,128)S(1)}, f32[8,64,128]{2,1,0:T(8,128)}, u32[]{:S(2)}) copy-start(f32[8,64,128]{2,1,0:T(8,128)} %refs_3_.1) | copy-start | bytes 786436
  0.7 9.2 %copy-start.2 = (f32[8,64,128]{2,1,0:T(8,128)S(1)}, f32[8,64,128]{2,1,0:T(8,128)}, u32[]{:S(2)}) copy-start(f32[8,64,128]{2,1,0:T(8,128)} %refs_2_.1) | copy-start | bytes 786436
  0.7 9.2 %copy-start.1 = (f32[8,64,128]{2,1,0:T(8,128)S(1)}, f32[8,64,128]{2,1,0:T(8,128)}, u32[]{:S(2)}) copy-start(f32[8,64,128]{2,1,0:T(8,128)} %refs_1_.1) | copy-start | bytes 786436
  0.7 9.2 %copy-start = (f32[8,64,128]{2,1,0:T(8,128)S(1)}, f32[8,64,128]{2,1,0:T(8,128)}, u32[]{:S(2)}) copy-start(f32[8,64,128]{2,1,0:T(8,128)} %refs_0_.1) | copy-start | bytes 786436
  2.0 14.2 %collective-permute-start.1 = (f32[27,8,128]{2,1,0:T(8,128)S(1)}, f32[27,8,128]{2,1,0:T(8,128)S(1)}, u32[]{:S(2)}, u32[]{:S(2)}) collective-permute-start(f32[27,8,128]{2,1,0:T(8,128)S(1)} %get-tuple-element.19), channel_id=1, source_target_pairs={{16,32},{17,33},{18,34},{19,35},{20,36},{21,37},{22,38},{23,39},{2... | collective-permute-start | bytes 331784 | tf_op jit(solution)/shard_map/ppermute | solution.py:553
  4.3 11.8 %collective-permute-start = (f32[21,8,128]{2,1,0:T(8,128)S(1)}, f32[21,8,128]{2,1,0:T(8,128)S(1)}, u32[]{:S(2)}, u32[]{:S(2)}) collective-permute-start(f32[21,8,128]{2,1,0:T(8,128)S(1)} %get-tuple-element.18), channel_id=1, source_target_pairs={{0,16},{1,17},{2,18},{3,19},{4,20},{5,21},{6,22},{7,23},{8,24},{9,... | collective-permute-start | bytes 258056 | tf_op jit(solution)/shard_map/ppermute | solution.py:554
  16.3 7.5 %collective-permute-start.2 = (f32[18,8,128]{2,1,0:T(8,128)S(1)}, f32[18,8,128]{2,1,0:T(8,128)S(1)}, u32[]{:S(2)}, u32[]{:S(2)}) collective-permute-start(f32[18,8,128]{2,1,0:T(8,128)S(1)} %get-tuple-element.20), channel_id=1, source_target_pairs={{0,15},{1,2},{2,1},{3,4},{4,3},{5,6},{6,5},{7,8},{8,7},{9,10},{10,... | collective-permute-start | bytes 221192 | tf_op jit(solution)/shard_map/ppermute | solution.py:564
  16.9 6.9 %collective-permute-start.3 = (f32[18,8,128]{2,1,0:T(8,128)S(1)}, f32[18,8,128]{2,1,0:T(8,128)S(1)}, u32[]{:S(2)}, u32[]{:S(2)}) collective-permute-start(f32[18,8,128]{2,1,0:T(8,128)S(1)} %get-tuple-element.21), channel_id=1, source_target_pairs={{0,1},{1,0},{2,3},{3,2},{4,5},{5,4},{6,7},{7,6},{8,9},{9,8},{10,11... | collective-permute-start | bytes 221192 | tf_op jit(solution)/shard_map/ppermute | solution.py:565

commit v5 on v4

--- a/solution.py
+++ b/solution.py
@@ -165,6 +165,8 @@
             copies.append(pltpu.make_async_copy(*pair, sems.at[f, side]))
     for copy in copies:
         copy.start()
+    for i in range(20, 27):
+        out_a[i] = jnp.ones((LEVELS, LANES), F32)
     out_b[25] = jnp.ones((LEVELS, LANES), F32)
     out_b[26] = jnp.ones((LEVELS, LANES), F32)
     for copy in copies:
@@ -287,7 +289,7 @@
         march(state, geo, ((2, ROWS - 2),))
         return carry
 
-    lax.fori_loop(1, NSTEP, step, 0)
+    lax.fori_loop(1, NSTEP - 1, step, 0)
 
 
 def columns_kernel(msgs, got_a, got_b, out_a, out_b):
@@ -325,10 +327,10 @@
 
 
 def rows_strip_kernel(*refs):
-    inner, inner_geo, rims, got_a, got_b, hinge, out, inner_out = refs[:8]
-    state = refs[8:12]
-    east_w, north_w = refs[12:14]
-    geo = dict(zip(GEO, refs[14:]))
+    inner, inner_geo, rims, got_a, got_b, hinge, out = refs[:7]
+    state = refs[7:11]
+    east_w, north_w = refs[11:13]
+    geo = dict(zip(GEO, refs[13:]))
     top = lax.axis_index("lat") == lax.axis_size("lat") - 1
     pivot = hinge[0]
     south, north, fold = halo_rows(got_a, got_b)
@@ -361,29 +363,34 @@
             chains.append((FOLD + s, 5 - s))
         march(state, geo, chains)
 
-    march(
-        [inner.at[f] for f in range(4)],
-        {name: inner_geo.at[index] for index, name in enumerate(GEO)},
-        ((HALO + 1, ROWS - 2 * HALO),),
-        [inner_out.at[f] for f in range(4)],
-    )
+    held = [out.at[f] for f in range(4)]
+    held_geo = {name: inner_geo.at[index] for index, name in enumerate(GEO)}
+    for f, ref in enumerate(held):
+        for row in range(HALO - 1, ROWS - HALO + 3):
+            ref[row] = inner[f, row]
+
+    def last(s, carry):
+        march(held, held_geo, ((HALO, ROWS - 2 * HALO + 2),))
+        return carry
+
+    lax.fori_loop(NSTEP - 1, NSTEP + 1, last, 0)
 
     for f, ref in enumerate(state):
         for i in range(HALO):
-            out[f, i] = ref[SOUTH + HALO + i]
-            out[f, HALO + i] = ref[NORTH + HALO + i]
+            out[f, 1 + i] = ref[SOUTH + HALO + i]
+            out[f, 1 + ROWS - HALO + i] = ref[NORTH + HALO + i]
 
 
 WEST, EAST, FOLDS, WE_ROWS = 0, 11, 22, 28
 
 
 def columns_strip_kernel(*refs):
-    own, lon_b, lon_a, got_a, got_b, inner, strips, hinge = refs[:8]
-    outs = refs[8:13]
-    state = refs[13:17]
-    east_w, north_w = refs[17:19]
-    geo = dict(zip(GEO, refs[19:29]))
-    stage, sems = refs[29:34], refs[34]
+    own, lon_b, lon_a, got_a, got_b, inner, hinge = refs[:7]
+    outs = refs[7:12]
+    state = refs[12:16]
+    east_w, north_w = refs[16:18]
+    geo = dict(zip(GEO, refs[18:28]))
+    stage, sems = refs[28:33], refs[33]
     even = lax.rem(lax.axis_index("lon"), 2) == 0
     top = lax.axis_index("lat") == lax.axis_size("lat") - 1
     below = hinge[0] == 1
@@ -469,11 +476,7 @@
     copies = []
     for row in range(ROWS):
         q, g = divmod(row + HALO, BLOCK)
-        if HALO <= row < ROWS - HALO:
-            bases = [inner[f, row + 1] for f in range(4)]
-        else:
-            place = row if row < HALO else row - (ROWS - 2 * HALO)
-            bases = [strips[f, place] for f in range(4)]
+        bases = [inner[f, row + 1] for f in range(4)]
         new = [
             jnp.where(rim, roll(ref[WEST + 1 + g], -(GROUP * q + HALO)), base) for ref, base in zip(state, bases)
         ]
@@ -543,7 +546,7 @@
     rows_a, rows_b = call(
         rows_kernel,
         fields,
-        [(21,) + tile, (27,) + tile],
+        [(27,) + tile, (27,) + tile],
         [pltpu.VMEM((2, LEVELS) + tile, kind) for kind in kinds[:6]]
         + [pltpu.VMEM((2,) + tile, F32)] * 2
         + [pltpu.SemaphoreType.DMA((8, 2))],
@@ -563,17 +566,17 @@
     pairs_a, pairs_b = lon_pairs(lat, lon)
     lon_b = lax.ppermute(cols_b, axes, pairs_b)
     lon_a = lax.ppermute(cols_a, axes, pairs_a)
-    strips, inner = call(
+    (inner,) = call(
         rows_strip_kernel,
         [inner, inner_geo, rims, got_a, got_b, hinge],
-        [(4, 2 * HALO) + tile, (4, ROWS + 2) + tile],
+        [(4, ROWS + 2) + tile],
         state_scratch(NS_ROWS) + geo_scratch(NS_ROWS),
         smem_last=True,
         flops=10_000_000,
     )
     outs = call(
         columns_strip_kernel,
-        [own, lon_b, lon_a, got_a, got_b, inner, strips, hinge],
+        [own, lon_b, lon_a, got_a, got_b, inner, hinge],
         [(LEVELS, ROWS, LANES)] * 5,
         state_scratch(WE_ROWS)
         + geo_scratch(WE_ROWS)

time: 28.3 us -> 27 us (0.954)
  the two profiles are of different devices: /device:TPU:48 before, /device:TPU:56 now
where the time goes in v5:
time: 27 us; the launch traced here: 26.9 us
  Pallas kernels  14 us (52%)
  starting transfers between devices  10.2 us (38%)
  between operations  1.46 us (5%)
  waiting for transfers between devices  1.14 us (4%)
    pallas_call x5, Pallas kernels, call(): pl.pallas_call(kernel, out_shape=out_shape, in_specs=specs, out_specs=[pl...  14 us
    ppermute x1, starting transfers between devices, on_device(): got_b = lax.ppermute(rows_b, axes, pairs_b)  6.23 us
    ppermute x1, starting transfers between devices, on_device(): lon_b = lax.ppermute(cols_b, axes, pairs_b)  3.18 us
    ppermute x1, waiting for transfers between devices, on_device(): lon_b = lax.ppermute(cols_b, axes, pairs_b)  0.83 us
    ppermute x1, starting transfers between devices, on_device(): got_a = lax.ppermute(rows_a, axes, pairs_a)  0.82 us
  transfers between devices with their start and end apart: 4, of which 2 were waited for; matrix products, arithmetic and copies ran while one was open for 0% of the time, Pallas kernels for 31%

profile of v5, /device:TPU:56, one launch (start us, length us, event | category | flops | bytes accessed | tf_op | source)
XLA Modules:
  0.0 26.9 jit_solution(9721168200320402057)
XLA Ops:
  0.6 0.0 copy-start.5
  0.6 0.0 copy-start.4
  0.7 0.0 copy-start.7
  0.7 0.0 copy-start.6
  0.7 0.0 copy-start.3
  0.7 0.0 copy-start.2
  0.7 0.0 copy-start.1
  0.7 0.0 copy-start
  0.7 1.2 %shard_map.129 = (f32[27,8,128]{2,1,0:T(8,128)S(1)}, f32[27,8,128]{2,1,0:T(8,128)S(1)}) custom-call(f32[8,64,128]{2,1,0:T(8,128)} %refs_0_.1, f32[8,64,128]{2,1,0:T(8,128)} %refs_1_.1, f32[8,64,128]{2,1,0:T(8,128)} %refs_2_.1, f32[8,64,128]{2,1,0:T(8,128)} %refs_3_.1, f32[8,64,128]{2,1,0:T(8,128)} %refs_4_.1, s32[8,64,128]{2,1,0:T(8,128)} %refs_5_.2, ...), custom_call_target="tpu_custom_call" | custom-call | bytes 2000000 | tf_op jit(solution)/shard_map/pallas_call | solution.py:508
  2.0 0.8 %collective-permute-start = (f32[27,8,128]{2,1,0:T(8,128)S(1)}, f32[27,8,128]{2,1,0:T(8,128)S(1)}, u32[]{:S(2)}, u32[]{:S(2)}) collective-permute-start(f32[27,8,128]{2,1,0:T(8,128)S(1)} %get-tuple-element.16), channel_id=1, source_target_pairs={{0,16},{1,17},{2,18},{3,19},{4,20},{5,21},{6,22},{7,23},{8,24},{9,... | collective-permute-start | bytes 331784 | tf_op jit(solution)/shard_map/ppermute | solution.py:557
  2.8 6.2 %collective-permute-start.1 = (f32[27,8,128]{2,1,0:T(8,128)S(1)}, f32[27,8,128]{2,1,0:T(8,128)S(1)}, u32[]{:S(2)}, u32[]{:S(2)}) collective-permute-start(f32[27,8,128]{2,1,0:T(8,128)S(1)} %get-tuple-element.17), channel_id=1, source_target_pairs={{16,32},{17,33},{18,34},{19,35},{20,36},{21,37},{22,38},{23,39},{2... | collective-permute-start | bytes 331784 | tf_op jit(solution)/shard_map/ppermute | solution.py:556
  9.0 0.0 copy-done.5
  9.0 0.0 copy-done.4
  9.0 0.0 copy-done.7
  9.0 0.0 copy-done.6
  9.1 0.0 copy-done.3
  9.1 0.0 copy-done.2
  9.1 0.0 copy-done.1
  9.1 0.0 copy-done
  9.1 5.5 %shard_map.128 = (f32[4,66,8,128]{3,2,1,0:T(8,128)S(1)}, f32[2,7,9,8,128]{4,3,2,1,0:T(8,128)S(1)}, f32[2,18,8,128]{3,2,1,0:T(8,128)S(1)}, f32[7,16,8,128]{3,2,1,0:T(8,128)S(1)}, f32[10,66,8,128]{3,2,1,0:T(8,128)S(1)}) custom-call(f32[512,128]{1,0:T(8,128)S(1)} %bitcast.6, f32[512,128]{1,0:T(8,128)S(1)} %bitcast.7, f32[512,128]{1,0:T(8,128)S(1)} %bitcast.8, ...), custom_call_target="tpu_custom_call" | custom-call | flops 40000000 | bytes 2000000 | tf_op jit(solution)/shard_map/pallas_call | solution.py:508
  14.6 0.0 collective-permute-done.got_a.refs_3_
  14.6 0.3 %collective-permute-done.1.got_b.refs_4_ = f32[27,8,128]{2,1,0:T(8,128)S(1)} collective-permute-done((f32[27,8,128]{2,1,0:T(8,128)S(1)}, f32[27,8,128]{2,1,0:T(8,128)S(1)}, u32[]{:S(2)}, u32[]{:S(2)}) %collective-permute-start.1) | collective-permute-done | bytes 110624 | tf_op jit(solution)/shard_map/ppermute | solution.py:556
  14.9 0.2 shard_map.130
  15.1 3.2 %collective-permute-start.2 = (f32[18,8,128]{2,1,0:T(8,128)S(1)}, f32[18,8,128]{2,1,0:T(8,128)S(1)}, u32[]{:S(2)}, u32[]{:S(2)}) collective-permute-start(f32[18,8,128]{2,1,0:T(8,128)S(1)} %get-tuple-element.18), channel_id=1, source_target_pairs={{0,15},{1,2},{2,1},{3,4},{4,3},{5,6},{6,5},{7,8},{8,7},{9,10},{10,... | collective-permute-start | bytes 221192 | tf_op jit(solution)/shard_map/ppermute | solution.py:567
  18.3 0.0 collective-permute-start.3
  18.9 2.8 %shard_map.131.refs_5_ = f32[4,66,8,128]{3,2,1,0:T(8,128)S(1)} custom-call(f32[4,66,8,128]{3,2,1,0:T(8,128)S(1)} %get-tuple-element.20.refs_0_, f32[10,66,8,128]{3,2,1,0:T(8,128)S(1)} %get-tuple-element.21.refs_1_, f32[7,16,8,128]{3,2,1,0:T(8,128)S(1)} %get-tuple-element.22.refs_2_, f32[27,8,128]{2,1,0:T(8,128)S(1)} %collective-permute-done.got_a.refs_3_, ...), custom_call_target="tpu_custom_call" | custom-call | flops 10000000 | bytes 2000000 | tf_op jit(solution)/shard_map/pallas_call | solution.py:508
  21.7 0.8 %collective-permute-done.2.refs_1_ = f32[18,8,128]{2,1,0:T(8,128)S(1)} collective-permute-done((f32[18,8,128]{2,1,0:T(8,128)S(1)}, f32[18,8,128]{2,1,0:T(8,128)S(1)}, u32[]{:S(2)}, u32[]{:S(2)}) %collective-permute-start.2) | collective-permute-done | bytes 73760 | tf_op jit(solution)/shard_map/ppermute | solution.py:567
  22.6 0.0 collective-permute-done.3.refs_2_
  22.6 4.3 %shard_map.132 = (f32[8,64,128]{2,1,0:T(8,128)}, f32[8,64,128]{2,1,0:T(8,128)}, f32[8,64,128]{2,1,0:T(8,128)}, f32[8,64,128]{2,1,0:T(8,128)}, f32[8,64,128]{2,1,0:T(8,128)}) custom-call(f32[2,7,9,8,128]{4,3,2,1,0:T(8,128)S(1)} %get-tuple-element.14.refs_0_, f32[18,8,128]{2,1,0:T(8,128)S(1)} %collective-permute-done.2.refs_1_, ...), custom_call_target="tpu_custom_call" | custom-call | flops 10000000 | bytes 2000000 | tf_op jit(solution)/shard_map/pallas_call | solution.py:508
Async XLA Ops:
  0.6 8.4 %copy-start.5 = (s32[8,64,128]{2,1,0:T(8,128)S(1)}, s32[8,64,128]{2,1,0:T(8,128)}, u32[]{:S(2)}) copy-start(s32[8,64,128]{2,1,0:T(8,128)} %refs_5_.2) | copy-start | bytes 786436
  0.6 8.4 %copy-start.4 = (f32[8,64,128]{2,1,0:T(8,128)S(1)}, f32[8,64,128]{2,1,0:T(8,128)}, u32[]{:S(2)}) copy-start(f32[8,64,128]{2,1,0:T(8,128)} %refs_4_.1) | copy-start | bytes 786436
  0.7 8.4 %copy-start.7 = (f32[64,128]{1,0:T(8,128)S(1)}, f32[64,128]{1,0:T(8,128)}, u32[]{:S(2)}) copy-start(f32[64,128]{1,0:T(8,128)} %refs_7_.3) | copy-start | bytes 98308
  0.7 8.4 %copy-start.6 = (f32[64,128]{1,0:T(8,128)S(1)}, f32[64,128]{1,0:T(8,128)}, u32[]{:S(2)}) copy-start(f32[64,128]{1,0:T(8,128)} %refs_6_.4) | copy-start | bytes 98308
  0.7 8.4 %copy-start.3 = (f32[8,64,128]{2,1,0:T(8,128)S(1)}, f32[8,64,128]{2,1,0:T(8,128)}, u32[]{:S(2)}) copy-start(f32[8,64,128]{2,1,0:T(8,128)} %refs_3_.1) | copy-start | bytes 786436
  0.7 8.4 %copy-start.2 = (f32[8,64,128]{2,1,0:T(8,128)S(1)}, f32[8,64,128]{2,1,0:T(8,128)}, u32[]{:S(2)}) copy-start(f32[8,64,128]{2,1,0:T(8,128)} %refs_2_.1) | copy-start | bytes 786436
  0.7 8.4 %copy-start.1 = (f32[8,64,128]{2,1,0:T(8,128)S(1)}, f32[8,64,128]{2,1,0:T(8,128)}, u32[]{:S(2)}) copy-start(f32[8,64,128]{2,1,0:T(8,128)} %refs_1_.1) | copy-start | bytes 786436
  0.7 8.4 %copy-start = (f32[8,64,128]{2,1,0:T(8,128)S(1)}, f32[8,64,128]{2,1,0:T(8,128)}, u32[]{:S(2)}) copy-start(f32[8,64,128]{2,1,0:T(8,128)} %refs_0_.1) | copy-start | bytes 786436
  2.0 12.6 %collective-permute-start = (f32[27,8,128]{2,1,0:T(8,128)S(1)}, f32[27,8,128]{2,1,0:T(8,128)S(1)}, u32[]{:S(2)}, u32[]{:S(2)}) collective-permute-start(f32[27,8,128]{2,1,0:T(8,128)S(1)} %get-tuple-element.16), channel_id=1, source_target_pairs={{0,16},{1,17},{2,18},{3,19},{4,20},{5,21},{6,22},{7,23},{8,24},{9,... | collective-permute-start | bytes 331784 | tf_op jit(solution)/shard_map/ppermute | solution.py:557
  2.8 12.1 %collective-permute-start.1 = (f32[27,8,128]{2,1,0:T(8,128)S(1)}, f32[27,8,128]{2,1,0:T(8,128)S(1)}, u32[]{:S(2)}, u32[]{:S(2)}) collective-permute-start(f32[27,8,128]{2,1,0:T(8,128)S(1)} %get-tuple-element.17), channel_id=1, source_target_pairs={{16,32},{17,33},{18,34},{19,35},{20,36},{21,37},{22,38},{23,39},{2... | collective-permute-start | bytes 331784 | tf_op jit(solution)/shard_map/ppermute | solution.py:556
  15.1 7.5 %collective-permute-start.2 = (f32[18,8,128]{2,1,0:T(8,128)S(1)}, f32[18,8,128]{2,1,0:T(8,128)S(1)}, u32[]{:S(2)}, u32[]{:S(2)}) collective-permute-start(f32[18,8,128]{2,1,0:T(8,128)S(1)} %get-tuple-element.18), channel_id=1, source_target_pairs={{0,15},{1,2},{2,1},{3,4},{4,3},{5,6},{6,5},{7,8},{8,7},{9,10},{10,... | collective-permute-start | bytes 221192 | tf_op jit(solution)/shard_map/ppermute | solution.py:567
  18.3 4.3 %collective-permute-start.3 = (f32[18,8,128]{2,1,0:T(8,128)S(1)}, f32[18,8,128]{2,1,0:T(8,128)S(1)}, u32[]{:S(2)}, u32[]{:S(2)}) collective-permute-start(f32[18,8,128]{2,1,0:T(8,128)S(1)} %get-tuple-element.19), channel_id=1, source_target_pairs={{0,1},{1,0},{2,3},{3,2},{4,5},{5,4},{6,7},{7,6},{8,9},{9,8},{10,11... | collective-permute-start | bytes 221192 | tf_op jit(solution)/shard_map/ppermute | solution.py:568
